TPU v7x, 256 devices: a whole 4x4x8 slice. The times are simulated.
256 devices in a mesh: aa: 16 (over x_lo, y, core), ba: 16 (over x_hi, z).
Axes of the slice: x: 4 (x_hi: 2, x_lo: 2; x = x_hi * 2 + x_lo), y: 4, z: 8, core: 2. Of those that a mesh axis runs over, the one named last changes fastest.
Arguments:
- pair_amplitude: bfloat16 [1024, 1024, 5, 128], P('aa', 'ba'), may hold values from -0.5 to 0.5
- row_amplitude: bfloat16 [1024, 2, 5, 128], P(('aa', 'ba')), may hold values from -0.5 to 0.5
- column_amplitude: bfloat16 [1024, 2, 5, 128], P(('ba', 'aa')), may hold values from -0.5 to 0.5
- row_integral: bfloat16 [1024, 3200], P(('aa', 'ba')), may hold values from -6 to 6
- column_integral: bfloat16 [1024, 3200], P(('ba', 'aa')), may hold values from -6 to 6
- step_integral: bfloat16 [2, 3200], replicated, may hold values from -6 to 6
- virtual_energy: float32 [1024], replicated, may hold values from 0.3 to 2
- occupied_energy: float32 [5], replicated, may hold values from -1.5 to -0.2
- step_energy: float32 [2], replicated, may hold values from 0.3 to 2
Outputs:
- row_residual: float32 [1024, 2, 5, 128], P(('aa', 'ba'))
- column_residual: float32 [1024, 2, 5, 128], P(('ba', 'aa'))
All inputs are finite; a program needn't handle non-finite values.
Results may differ from a plain program's by a relative error of at most 0.0005.
Values may be sent and summed in bfloat16 or wider, within the bound.
A program may use at most 64 MiB of HBM per device.

v0:
```python
import math

import jax
import jax.numpy as jnp
from jax import lax
from jax.sharding import PartitionSpec as P


def on_device(
    pair_amplitude,
    row_amplitude,
    column_amplitude,
    row_integral,
    column_integral,
    step_integral,
    virtual_energy,
    occupied_energy,
    step_energy,
):
    tile_rows, tile_columns, tile_size, all_occupied = pair_amplitude.shape
    step_count = row_amplitude.shape[1]
    virtual_count = tile_rows * lax.axis_size("aa")
    factor = 1.0 / (math.sqrt(virtual_count) * tile_size)
    row_energy = lax.dynamic_slice_in_dim(
        virtual_energy, lax.axis_index("aa") * tile_rows, tile_rows
    )
    column_energy = lax.dynamic_slice_in_dim(
        virtual_energy, lax.axis_index("ba") * tile_columns, tile_columns
    )
    occupied_sum = (
        occupied_energy[:, None, None]
        + occupied_energy[None, :, None]
        + occupied_energy[None, None, :]
    )
    step_table = step_integral.reshape(step_count, all_occupied, tile_size, tile_size)
    lead_whole, lead_table_whole = (
        lax.all_gather(row_amplitude, "ba", axis=0, tiled=True),
        lax.all_gather(row_integral, "ba", axis=0, tiled=True),
    )
    tail_whole, tail_table_whole = (
        lax.all_gather(column_amplitude, "aa", axis=0, tiled=True),
        lax.all_gather(column_integral, "aa", axis=0, tiled=True),
    )
    row_list = []
    column_list = []
    for which in range(step_count):
        lead_step = lead_whole[:, which]
        tail_step = tail_whole[:, which]
        lead_count = lead_step.shape[0]
        tail_count = tail_step.shape[0]
        sub_rows = math.gcd(lead_count, 4)
        turns = lead_count // sub_rows
        pair_parts = pair_amplitude.reshape(turns, sub_rows, tail_count, tile_size, all_occupied)
        lead_parts = lead_step.reshape(turns, sub_rows, tile_size, all_occupied)
        lead_tables = lead_table_whole.reshape(turns, sub_rows, all_occupied, tile_size, tile_size)
        tail_table = tail_table_whole.reshape(tail_count, all_occupied, tile_size, tile_size)
        lead_energies = row_energy.reshape(turns, sub_rows)
        table = step_table[which]

        def one_turn(column_total, pieces):
            pair_piece, lead_piece, lead_table, lead_energy = pieces
            triples = jnp.einsum(
                "abil,ljk->abijk", pair_piece, table, preferred_element_type=jnp.float32
            )
            triples = triples + jnp.einsum(
                "abjl,lki->abijk", pair_piece, table, preferred_element_type=jnp.float32
            )
            triples = triples + jnp.einsum(
                "ail,bljk->abijk", lead_piece, tail_table, preferred_element_type=jnp.float32
            )
            triples = triples + jnp.einsum(
                "akl,blij->abijk", lead_piece, tail_table, preferred_element_type=jnp.float32
            )
            triples = triples + jnp.einsum(
                "bjl,alki->abijk", tail_step, lead_table, preferred_element_type=jnp.float32
            )
            triples = triples + jnp.einsum(
                "bkl,alij->abijk", tail_step, lead_table, preferred_element_type=jnp.float32
            )
            denominator = (
                lead_energy[:, None, None, None, None]
                + column_energy[None, :, None, None, None]
                + step_energy[which]
                - occupied_sum[None, None]
            )
            weighted = (triples / denominator).astype(jnp.bfloat16)
            row_part = jnp.einsum(
                "abijk,bljk->ail", weighted, tail_table, preferred_element_type=jnp.float32
            )
            column_part = jnp.einsum(
                "abijk,alki->bjl", weighted, lead_table, preferred_element_type=jnp.float32
            )
            return (column_total + column_part, row_part)

        column_start_total = jnp.zeros((tail_count, tile_size, all_occupied), jnp.float32)
        column_part, row_parts = lax.scan(
            one_turn, column_start_total, (pair_parts, lead_parts, lead_tables, lead_energies)
        )
        row_total = row_parts.reshape(lead_count, tile_size, all_occupied)
        column_total = column_part
        row_list.append(row_total)
        column_list.append(column_total)
    row_residual = (
        lax.psum_scatter(jnp.stack(row_list, 1), "ba", scatter_dimension=0, tiled=True) * factor
    )
    column_residual = (
        lax.psum_scatter(jnp.stack(column_list, 1), "aa", scatter_dimension=0, tiled=True) * factor
    )
    return (row_residual, column_residual)


def solution(mesh):
    placed = (
        P("aa", "ba", None, None),
        P(("aa", "ba"), None, None, None),
        P(("ba", "aa"), None, None, None),
        P(("aa", "ba"), None),
        P(("ba", "aa"), None),
        P(),
        P(),
        P(),
        P(),
    )
    return jax.shard_map(
        on_device,
        mesh=mesh,
        in_specs=placed,
        out_specs=(P(("aa", "ba"), None, None, None), P(("ba", "aa"), None, None, None)),
        check_vma=False,
    )
```

profile of v0, /device:TPU:1, one launch (start us, length us, event | category | flops | bytes accessed | tf_op | source)
XLA Modules:
  0.0 559.9 jit_solution(6067093046884766947)
XLA Ops:
  8.2 21.9 %all_gather.15 = bf16[64,2,5,128]{3,1,2,0:T(2,128)(2,1)S(1)} all-gather(bf16[4,2,5,128]{3,1,2,0:T(2,128)(2,1)} %param.15), channel_id=1, replica_groups=mesh['aa'=16,'ba'=16] {'aa'}, dimensions={0}, use_global_device_ids=true | all-gather | bytes 174080 | tf_op jit(solution)/shard_map/all_gather | solution.py:41
  30.3 17.6 %all-gather = bf16[16,4,3200]{2,1,0:T(4,128)(2,1)S(1)} all-gather(bf16[1,4,3200]{2,1,0:T(4,128)(2,1)} %bitcast.251), channel_id=1, replica_groups=mesh['aa'=16,'ba'=16] {'aa'}, dimensions={0}, use_global_device_ids=true | all-gather | bytes 435200 | tf_op jit(solution)/shard_map/all_gather | solution.py:42
  47.9 10.7 %copy.101 = bf16[16,4,3200]{1,0,2:T(8,128)(2,1)} copy(bf16[16,4,3200]{2,1,0:T(4,128)(2,1)S(1)} %all-gather) | data formatting | bytes 819200 | tf_op jit(solution)/shard_map/all_gather | solution.py:42
  58.6 16.6 %reshape.137 = bf16[64,128,5,5]{0,3,2,1:T(8,128)(2,1)S(1)} reshape(bf16[16,4,3200]{1,0,2:T(8,128)(2,1)} %copy.101) | data formatting | bytes 819200 | tf_op jit(solution)/shard_map/reshape | solution.py:56
  76.6 38.8 %all-gather.1 = bf16[16,4,3200]{2,1,0:T(4,128)(2,1)S(1)} all-gather(bf16[1,4,3200]{2,1,0:T(4,128)(2,1)S(1)} %bitcast.252), channel_id=1, replica_groups=mesh['aa'=16,'ba'=16] {'ba'}, dimensions={0}, use_global_device_ids=true | all-gather | bytes 435200 | tf_op jit(solution)/shard_map/all_gather | solution.py:38
  115.4 3.6 copy.102
  118.9 5.5 copy.107
  124.4 29.9 %all_gather.12 = bf16[64,2,5,128]{3,1,2,0:T(2,128)(2,1)S(1)} all-gather(bf16[4,2,5,128]{3,1,2,0:T(2,128)(2,1)S(1)} %copy-done.4), channel_id=1, replica_groups=mesh['aa'=16,'ba'=16] {'ba'}, dimensions={0}, use_global_device_ids=true | all-gather | bytes 174080 | tf_op jit(solution)/shard_map/all_gather | solution.py:37
  155.2 51.4 %while.26 = (s32[]{:T(128)}, f32[64,5,128]{2,0,1:T(8,128)S(1)}, f32[16,4,5,128]{3,1,0,2:T(4,128)S(1)}, bf16[16,4,64,5,128]{4,2,3,1,0:T(8,128)(2,1)}, bf16[128,5,...) while((s32[]{:T(128)}, f32[64,5,128]{2,0,1:T(8,128)S(1)}, ...), condition=%wide.region_1.2_spmd.clone, body=%wide.region_0.1_spmd.clone.sunk | while | flops 41298556 | bytes 2697031 | solution.py:96
  162.5 1.4 fusion.87
  172.1 1.4 fusion.87
  181.8 1.4 fusion.87
  191.4 1.4 fusion.87
  201.1 1.4 fusion.87
  207.2 70.3 %while.27 = (s32[]{:T(128)}, f32[64,5,128]{2,0,1:T(8,128)S(1)}, f32[16,4,5,128]{3,1,0,2:T(4,128)S(1)}, bf16[16,4,64,5,128]{4,2,3,1,0:T(8,128)(2,1)}, bf16[128,5,...) while((s32[]{:T(128)}, f32[64,5,128]{2,0,1:T(8,128)S(1)}, ...), condition=%wide.region_3.4_spmd.clone, body=%wide.region_2.3_spmd.clone.sunk | while | flops 41298556 | bytes 2697039 | solution.py:96
  209.2 1.4 fusion.102
  213.6 1.4 fusion.102
  218.0 1.4 fusion.102
  222.4 1.4 fusion.102
  226.8 1.4 fusion.102
  231.2 1.4 fusion.102
  235.6 1.4 fusion.102
  240.0 1.4 fusion.102
  244.4 1.4 fusion.102
  248.8 1.4 fusion.102
  253.2 1.4 fusion.102
  257.6 1.4 fusion.102
  261.9 1.4 fusion.102
  266.3 1.4 fusion.102
  270.7 1.4 fusion.102
  281.6 122.8 %all-reduce.7.cloned.1.call-done = f32[64,2,5,128]{3,0,2,1:T(8,128)} async-done(((f32[64,2,5,128]{3,0,2,1:T(8,128)}), f32[64,2,5,128]{3,0,2,1:T(8,128)}) %all-reduce.7.cloned.1.call-update) | async-done | bytes 327696
  405.8 145.9 %all-reduce.5.cloned.1.call-done = f32[64,2,5,128]{3,0,2,1:T(8,128)} async-done(((f32[64,2,5,128]{3,0,2,1:T(8,128)}), f32[64,2,5,128]{3,0,2,1:T(8,128)}) %all-reduce.5.cloned.1.call-update) | async-done | bytes 327696
  (424 shorter events, 101.7 us)
Async XLA Ops:
  7.2 397.3 %all-reduce.7.cloned.1.call-start = ((), (), s32[]{:S(2)}) async-start(), calls=%async_computation.1 | async-start | bytes 655360
  58.6 18.0 %copy-start.2 = (bf16[4,3200]{1,0:T(4,128)(2,1)S(1)}, bf16[4,3200]{1,0:T(4,128)(2,1)}, u32[]{:S(2)}) copy-start(bf16[4,3200]{1,0:T(4,128)(2,1)} %param.16) | copy-start | bytes 76804
  75.2 49.2 %copy-start.4 = (bf16[4,2,5,128]{3,1,2,0:T(2,128)(2,1)S(1)}, bf16[4,2,5,128]{3,1,2,0:T(2,128)(2,1)}, u32[]{:S(2)}) copy-start(bf16[4,2,5,128]{3,1,2,0:T(2,128)(2,1)} %param.14) | copy-start | bytes 30724
  75.2 79.3 %copy-start.1 = (bf16[2,3200]{1,0:T(2,128)(2,1)S(1)}, bf16[2,3200]{1,0:T(2,128)(2,1)}, u32[]{:S(2)}) copy-start(bf16[2,3200]{1,0:T(2,128)(2,1)} %param.18) | copy-start | bytes 38404
  76.5 78.5 %copy-start = (f32[5]{0:T(128)S(1)}, f32[5]{0:T(128)}, u32[]{:S(2)}) copy-start(f32[5]{0:T(128)} %param.20) | copy-start | bytes 64
  76.6 78.7 %copy-start.3 = (f32[2]{0:T(128)S(1)}, f32[2]{0:T(128)}, u32[]{:S(2)}) copy-start(f32[2]{0:T(128)} %param.21) | copy-start | bytes 28
  207.2 72.0 %copy-start.6 = (u32[256]{0:T(256)S(1)}, u32[256]{0:T(256)}, u32[]{:S(2)}) copy-start(u32[256]{0:T(256)} %constant.53) | copy-start | bytes 3076
  207.2 72.6 %copy-start.5 = (u32[256]{0:T(256)S(1)}, u32[256]{0:T(256)}, u32[]{:S(2)}) copy-start(u32[256]{0:T(256)} %constant.49) | copy-start | bytes 3076
  278.3 273.4 %all-reduce.5.cloned.1.call-start = ((), (), s32[]{:S(2)}) async-start(), calls=%async_computation | async-start | bytes 655360
Sparse Core Ops, SparseCore 0:
  278.4 125.9 all-reduce.6
  407.2 144.4 all-reduce.4
where the time goes:
time: 571 us; the launch traced here: 560 us
  waiting for transfers between devices  269 us (47%)
  blocking collectives  108 us (19%)
  matrix products  82.4 us (14%)
  local copies, waits for them, and re-layouts  53.6 us (9%)
  other arithmetic  29.2 us (5%)
  between operations  15.6 us (3%)
    unnamed x4, waiting for transfers between devices  269 us
    dot_general x32, matrix products, one_turn(): jnp.einsum('abil,ljk->abijk', pair_piece, table, preferred_element_type=j...  43.6 us
    all_gather x1, blocking collectives, on_device(): lax.all_gather(row_integral, 'ba', axis=0, tiled=True)  38.8 us
    all_gather x1, blocking collectives, on_device(): lax.all_gather(row_amplitude, 'ba', axis=0, tiled=True)  29.9 us
    all_gather x1, blocking collectives, on_device(): lax.all_gather(column_amplitude, 'aa', axis=0, tiled=True)  21.9 us
    all_gather x1, blocking collectives, on_device(): lax.all_gather(column_integral, 'aa', axis=0, tiled=True)  17.6 us
    reshape x1, local copies, waits for them, and re-layouts, on_device(): tail_table_whole.reshape(tail_count, all_occupied, tile_size, tile_size)  16.6 us
    dot_general x32, matrix products, one_turn(): jnp.einsum('ail,bljk->abijk', lead_piece, tail_table, preferred_element_t...  14 us
  transfers between devices with their start and end apart: 2, of which 2 were waited for; matrix products, arithmetic and copies ran while one was open for 1% of the time, Pallas kernels for 0%

commit v1 on v0

v1 whole, which is shorter than its diff:
```python
import functools
import math

import jax
import jax.numpy as jnp
from jax import lax
from jax.experimental import pallas as pl
from jax.experimental.pallas import tpu as pltpu
from jax.sharding import PartitionSpec as P

F32 = jnp.float32
BF16 = jnp.bfloat16
MESH = pl.DeviceIdType.MESH
GROUP = 16
OWN = 4
OT = 5
JK = OT * OT
NC = 2
SI = OT * NC
NO = 128
CHUNK = 144
PART = 40
AROWS = 56
NT = (((1,), (1,)), ((), ()))


def dot_nt(x, y):
    return lax.dot_general(x, y, NT, preferred_element_type=F32)


def split_l(g_ref, h_ref, q_ref, r_ref, u_ref, row_chunk, col_chunk, q_out, amp):
    top = jnp.concatenate([g_ref[...].astype(F32), h_ref[...].astype(F32)], 0)
    low = jnp.concatenate(
        [q_ref[...].astype(F32), jnp.zeros((6, JK * NO), F32)], 0
    )
    row = lax.broadcasted_iota(jnp.int32, (NO, NO), 0)
    col = lax.broadcasted_iota(jnp.int32, (NO, NO), 1)
    perm = (row == ((JK * col) & 127)).astype(F32).astype(BF16)
    stacked = jnp.concatenate(
        [
            part[:, m * NO : (m + 1) * NO]
            for m in range(JK)
            for part in (top, low)
        ],
        0,
    ).astype(BF16)
    moved = jnp.dot(stacked, perm, preferred_element_type=F32)
    lane = lax.broadcasted_iota(jnp.int32, (8, NO), 1)
    tops, lows = [], []
    for jk in range(JK):
        source = (JK * ((lane - 41 * jk) & 127) + jk) >> 7
        t = moved[0:8]
        w = moved[8:16]
        for m in range(1, JK):
            mask = source == m
            t = jnp.where(mask, moved[16 * m : 16 * m + 8], t)
            w = jnp.where(mask, moved[16 * m + 8 : 16 * m + 16], w)
        shift = (-41 * jk) % 128
        if shift:
            t = pltpu.roll(t, shift, 1)
            w = pltpu.roll(w, shift, 1)
        tops.append(t)
        lows.append(w)
    for which, (src, dst) in enumerate(((r_ref, row_chunk), (u_ref, col_chunk))):
        amp[...] = src[...].astype(F32)
        pieces = [t[4 * which : 4 * which + 4] for t in tops]
        pieces += [amp[pl.ds(c, OWN, stride=SI), :] for c in range(SI)]
        pieces.append(jnp.zeros((4, NO), F32))
        for k in range(9):
            dst[16 * k : 16 * k + 16, :] = jnp.concatenate(
                pieces[4 * k : 4 * k + 4], 0
            ).astype(BF16)
    rows = [lows[jk][s : s + 1] for s in range(NC) for jk in range(JK)]
    rows.append(jnp.zeros((64 - NC * JK, NO), F32))
    q_out[...] = jnp.concatenate(rows, 0).astype(BF16)


def gather_body(
    g_ref, h_ref, q_ref, r_ref, u_ref, rows_ref, cols_ref, q_out,
    row_chunk, col_chunk, amp, send_sems, row_sems, col_sems, own_sems,
):
    me_a = lax.axis_index("aa")
    me_b = lax.axis_index("ba")
    barrier = pltpu.get_barrier_semaphore()
    for step in range(1, GROUP):
        pl.semaphore_signal(
            barrier, inc=1, device_id=(me_a, lax.rem(me_b + step, GROUP)),
            device_id_type=MESH,
        )
        pl.semaphore_signal(
            barrier, inc=1, device_id=(lax.rem(me_a + step, GROUP), me_b),
            device_id_type=MESH,
        )
    split_l(g_ref, h_ref, q_ref, r_ref, u_ref, row_chunk, col_chunk, q_out, amp)
    pl.semaphore_wait(barrier, 2 * (GROUP - 1))
    copies = []
    for step in range(1, GROUP):
        for which, (src, dst, sems, at, target) in enumerate(
            (
                (row_chunk, rows_ref, row_sems, me_b, (me_a, lax.rem(me_b + step, GROUP))),
                (col_chunk, cols_ref, col_sems, me_a, (lax.rem(me_a + step, GROUP), me_b)),
            )
        ):
            copy = pltpu.make_async_remote_copy(
                src_ref=src,
                dst_ref=dst.at[pl.ds(at * CHUNK, CHUNK), :],
                send_sem=send_sems.at[which, step],
                recv_sem=sems.at[step],
                device_id=target,
                device_id_type=MESH,
            )
            copy.start()
            copies.append(copy)
    own = [
        pltpu.make_async_copy(
            row_chunk, rows_ref.at[pl.ds(me_b * CHUNK, CHUNK), :], own_sems.at[0]
        ),
        pltpu.make_async_copy(
            col_chunk, cols_ref.at[pl.ds(me_a * CHUNK, CHUNK), :], own_sems.at[1]
        ),
    ]
    for copy in own:
        copy.start()
    for copy in own:
        copy.wait()
    for copy in copies:
        copy.wait()


def spread(src, wide, kind):
    for k in range(9):
        blocks = [
            src[e * CHUNK + 16 * k : e * CHUNK + 16 * k + 16, :].astype(F32)
            for e in range(GROUP)
        ]
        for c in range(4):
            at = 4 * k + c
            if at >= JK + SI:
                continue
            tile = jnp.concatenate([b[4 * c : 4 * c + 4] for b in blocks], 0)
            wide(at, tile.astype(BF16))


def compute_a(t_ref, q_ref, a_out):
    q = q_ref[0:AROWS, :]

    def pair(n, _):
        for i in range(OT):
            block = jnp.concatenate(
                [
                    t_ref[2 * n, i], t_ref[2 * n + 32, i],
                    t_ref[2 * n + 1, i], t_ref[2 * n + 33, i],
                ],
                0,
            )
            part = dot_nt(q, block)
            for half in range(2):
                at = pl.multiple_of((2 * n + half) * (OT * AROWS) + i * AROWS, 8)
                a_out[pl.ds(at, AROWS), :] = part[:, half * NO : (half + 1) * NO]
        return 0

    lax.fori_loop(0, 16, pair, 0)


def put_rows(g2, r2, at, tile):
    dst, c = (g2, at) if at < JK else (r2, at - JK)
    dst[c * 32 : c * 32 + 32, 0:NO] = tile[0:32]
    dst[c * 32 : c * 32 + 32, NO : 2 * NO] = tile[32:64]


def put_cols(bdh, bdu, at, tile):
    dst, c = (bdh, at) if at < JK else (bdu, at - JK)
    dst[c * NO : c * NO + 64, 0:NO] = tile
    dst[c * NO + 64 : c * NO + NO, NO : 2 * NO] = tile


def clear_off(bdh, bdu):
    zero = jnp.zeros((64, NO), BF16)
    for dst, count in ((bdh, JK), (bdu, SI)):
        for c in range(count):
            dst[c * NO : c * NO + 64, NO : 2 * NO] = zero
            dst[c * NO + 64 : c * NO + NO, 0:NO] = zero


def pair_energy(ve_ref, me_a, me_b):
    lane = lax.broadcasted_iota(jnp.int32, (32, NO), 1)
    row = lax.broadcasted_iota(jnp.int32, (32, NO), 0)
    lead = jnp.broadcast_to(ve_ref[pl.ds(me_a // 2, 1), :], (32, NO))
    first = lax.rem(me_a, 2) * 64
    halves = [
        jnp.sum(
            jnp.where(lane == first + 32 * half + row, lead, 0.0), 1, keepdims=True
        )
        for half in range(2)
    ]
    tail = ve_ref[pl.ds(me_b // 2, 1), :]
    turned = pltpu.roll(jnp.broadcast_to(tail, (8, NO)), 64, 1)[0:1]
    lane1 = lane[0:1]
    keep = (lane1 // 64) == lax.rem(me_b, 2)
    tail = jnp.where(keep, tail, turned)
    return jnp.where(lane < 64, halves[0], halves[1]) + tail


def compute_pc(g2, r2, bdh, bdu, p_out, c_out):
    r = r2[...]

    for n in range(JK // 2 + 1):
        width = 2 if n < JK // 2 else 1
        part = dot_nt(r, bdh[2 * n * NO : (2 * n + width) * NO, :])
        for half in range(width):
            p_out[(2 * n + half) * 320 : (2 * n + half + 1) * 320, :] = part[
                :, half * NO : (half + 1) * NO
            ]
    for n in range(OT):
        for m in range(5):
            part = dot_nt(
                g2[m * 160 : (m + 1) * 160, :], bdu[2 * n * NO : (2 * n + 2) * NO, :]
            )
            for half in range(2):
                at = (2 * n + half) * 800 + m * 160
                c_out[at : at + 160, :] = part[:, half * NO : (half + 1) * NO]


def weigh(oe_ref, se_ref, base, a_in, p_in, c_in, yr, yc):
    def one(n, _):
        i = n // NC
        s = lax.rem(n, NC)
        start = base + se_ref[s]
        for j in range(OT):
            for k in range(OT):
                jk = j * OT + k
                ki = k * OT + i
                ij = i * OT + j
                energy = (oe_ref[i] + oe_ref[j]) + oe_ref[k]
                tiles = []
                for v in range(4):
                    first = v * 8 * OT * AROWS + s * JK
                    w = a_in[pl.ds(first + i * AROWS + jk, 8, stride=OT * AROWS), :]
                    w = w + a_in[pl.ds(first + j * AROWS + ki, 8, stride=OT * AROWS), :]
                    at = pl.multiple_of(jk * 320 + (i * NC + s) * 32 + v * 8, 8)
                    w = w + p_in[pl.ds(at, 8), :]
                    at = pl.multiple_of(ij * 320 + (k * NC + s) * 32 + v * 8, 8)
                    w = w + p_in[pl.ds(at, 8), :]
                    at = pl.multiple_of((j * NC + s) * 800 + ki * 32 + v * 8, 8)
                    w = w + c_in[pl.ds(at, 8), :]
                    at = pl.multiple_of((k * NC + s) * 800 + ij * 32 + v * 8, 8)
                    w = w + c_in[pl.ds(at, 8), :]
                    tiles.append(w / (start[v * 8 : v * 8 + 8] - energy))
                y = jnp.concatenate(tiles, 0).astype(BF16)
                at = pl.multiple_of((i * NC + s) * 32, 32)
                yr[pl.ds(at, 32), jk * NO : (jk + 1) * NO] = y
                at = pl.multiple_of((j * NC + s) * 800 + ki * 32, 32)
                yc[pl.ds(at, 32), :] = y
        return 0

    lax.fori_loop(0, SI, one, 0)


def residuals(g2, bdh, yr, yc, res, row_out, col_out):
    out = jnp.dot(yr[...], bdh[...], preferred_element_type=F32)
    for c in range(SI):
        for half in range(2):
            res[c * 64 + half * 32 : c * 64 + half * 32 + 32, :] = out[
                c * 32 : c * 32 + 32, half * NO : (half + 1) * NO
            ]
    for c in range(SI):
        for v in range(OWN):
            row_out[pl.ds(v * SI + c, GROUP, stride=PART), :] = res[
                pl.ds(c * 64 + v, GROUP, stride=OWN), :
            ]
    turned = g2[...].T
    lane = lax.broadcasted_iota(jnp.int32, (NO, NO), 1)
    for n in range(OT):
        wide = jnp.concatenate(
            [yc[(2 * n + half) * 800 : (2 * n + half + 1) * 800, :] for half in range(2)], 1
        )
        out = jnp.dot(turned, wide, preferred_element_type=F32)
        for half in range(2):
            piece = out[:, half * NO : (half + 1) * NO]
            both = jnp.where(lane < 64, piece[0:NO], piece[NO:]).T
            at = (2 * n + half) * 64
            res[at : at + 64, :] = both[0:64] + both[64:128]
    for c in range(SI):
        for v in range(OWN):
            col_out[pl.ds(v * SI + c, GROUP, stride=PART), :] = res[
                pl.ds(c * 64 + v, GROUP, stride=OWN), :
            ]


def compute_body(
    t_hbm, q_ref, rows_ref, cols_ref, ve_ref, oe_ref, se_ref, row_out, col_out,
    t_ref, a_ref, g2, r2, bdh, bdu, p_ref, c_ref, yr, yc, res, t_sem,
):
    copy = pltpu.make_async_copy(t_hbm, t_ref, t_sem)
    copy.start()
    clear_off(bdh, bdu)
    spread(rows_ref, functools.partial(put_rows, g2, r2), 0)
    spread(cols_ref, functools.partial(put_cols, bdh, bdu), 1)
    compute_pc(g2, r2, bdh, bdu, p_ref, c_ref)
    copy.wait()
    compute_a(t_ref, q_ref, a_ref)
    base = pair_energy(ve_ref, lax.axis_index("aa"), lax.axis_index("ba"))
    weigh(oe_ref, se_ref, base, a_ref, p_ref, c_ref, yr, yc)
    residuals(g2, bdh, yr, yc, res, row_out, col_out)


def compute_call(t, q, rows, cols, ve, oe, se):
    vm = pl.BlockSpec(memory_space=pltpu.VMEM)
    sm = pl.BlockSpec(memory_space=pltpu.SMEM)
    shape = jax.ShapeDtypeStruct((GROUP * PART, NO), F32)
    return pl.pallas_call(
        compute_body,
        out_shape=(shape, shape),
        in_specs=[pl.BlockSpec(memory_space=pl.ANY), vm, vm, vm, vm, sm, sm],
        out_specs=(vm, vm),
        scratch_shapes=[
            pltpu.VMEM((64, OT, 64, NO), BF16),
            pltpu.VMEM((32 * OT * AROWS, NO), F32),
            pltpu.VMEM((JK * 32, 2 * NO), BF16),
            pltpu.VMEM((SI * 32, 2 * NO), BF16),
            pltpu.VMEM((JK * NO, 2 * NO), BF16),
            pltpu.VMEM((SI * NO, 2 * NO), BF16),
            pltpu.VMEM((JK * 320, NO), F32),
            pltpu.VMEM((SI * 800, NO), F32),
            pltpu.VMEM((320, JK * NO), BF16),
            pltpu.VMEM((SI * 800, NO), BF16),
            pltpu.VMEM((SI * 64, NO), F32),
            pltpu.SemaphoreType.DMA,
        ],
        compiler_params=pltpu.CompilerParams(vmem_limit_bytes=48 * 2**20),
    )(t, q, rows, cols, ve, oe, se)


def scatter_body(
    factor, row_ref, col_ref, row_out, col_out, row_in, col_in, send_sems, row_sems, col_sems
):
    me_a = lax.axis_index("aa")
    me_b = lax.axis_index("ba")
    barrier = pltpu.get_barrier_semaphore()
    for step in range(1, GROUP):
        pl.semaphore_signal(
            barrier, inc=1, device_id=(me_a, lax.rem(me_b + step, GROUP)),
            device_id_type=MESH,
        )
        pl.semaphore_signal(
            barrier, inc=1, device_id=(lax.rem(me_a + step, GROUP), me_b),
            device_id_type=MESH,
        )
    pl.semaphore_wait(barrier, 2 * (GROUP - 1))
    copies = []
    for step in range(1, GROUP):
        to_b = lax.rem(me_b + step, GROUP)
        to_a = lax.rem(me_a + step, GROUP)
        for which, (src, dst, sems, at, target) in enumerate(
            (
                (row_ref, row_in, row_sems, to_b, (me_a, to_b)),
                (col_ref, col_in, col_sems, to_a, (to_a, me_b)),
            )
        ):
            copy = pltpu.make_async_remote_copy(
                src_ref=src.at[pl.ds(at * PART, PART), :],
                dst_ref=dst.at[step],
                send_sem=send_sems.at[which, step],
                recv_sem=sems.at[step],
                device_id=target,
                device_id_type=MESH,
            )
            copy.start()
            copies.append(copy)
    row_sum = row_ref[pl.ds(me_b * PART, PART), :]
    col_sum = col_ref[pl.ds(me_a * PART, PART), :]
    for n, copy in enumerate(copies):
        copy.wait_recv()
        if n % 2 == 0:
            row_sum = row_sum + row_in[n // 2 + 1]
        else:
            col_sum = col_sum + col_in[n // 2 + 1]
    row_out[...] = row_sum * factor
    col_out[...] = col_sum * factor
    for copy in copies:
        copy.wait_send()


def on_device(
    pair_amplitude,
    row_amplitude,
    column_amplitude,
    row_integral,
    column_integral,
    step_integral,
    virtual_energy,
    occupied_energy,
    step_energy,
):
    vm = pl.BlockSpec(memory_space=pltpu.VMEM)
    factor = 1.0 / (math.sqrt(virtual_energy.shape[0]) * OT)
    t = pair_amplitude.transpose(0, 2, 1, 3)
    r = row_amplitude.transpose(0, 2, 1, 3).reshape(PART, NO)
    u = column_amplitude.transpose(0, 2, 1, 3).reshape(PART, NO)
    whole = jax.ShapeDtypeStruct((GROUP * CHUNK, NO), BF16)
    rows, cols, q = pl.pallas_call(
        gather_body,
        out_shape=(whole, whole, jax.ShapeDtypeStruct((64, NO), BF16)),
        in_specs=[vm] * 5,
        out_specs=(vm, vm, vm),
        scratch_shapes=[
            pltpu.VMEM((CHUNK, NO), BF16),
            pltpu.VMEM((CHUNK, NO), BF16),
            pltpu.VMEM((PART, NO), F32),
            pltpu.SemaphoreType.DMA((2, GROUP)),
            pltpu.SemaphoreType.DMA((GROUP,)),
            pltpu.SemaphoreType.DMA((GROUP,)),
            pltpu.SemaphoreType.DMA((2,)),
        ],
        compiler_params=pltpu.CompilerParams(
            collective_id=0, has_side_effects=True, vmem_limit_bytes=32 * 2**20
        ),
    )(row_integral, column_integral, step_integral, r, u)
    row_part, col_part = compute_call(
        t, q, rows, cols, virtual_energy.reshape(8, NO), occupied_energy, step_energy
    )
    part = jax.ShapeDtypeStruct((PART, NO), F32)
    row_res, col_res = pl.pallas_call(
        functools.partial(scatter_body, factor),
        out_shape=(part, part),
        in_specs=[vm] * 2,
        out_specs=(vm, vm),
        scratch_shapes=[
            pltpu.VMEM((GROUP, PART, NO), F32),
            pltpu.VMEM((GROUP, PART, NO), F32),
            pltpu.SemaphoreType.DMA((2, GROUP)),
            pltpu.SemaphoreType.DMA((GROUP,)),
            pltpu.SemaphoreType.DMA((GROUP,)),
        ],
        compiler_params=pltpu.CompilerParams(
            collective_id=1, has_side_effects=True, vmem_limit_bytes=32 * 2**20
        ),
    )(row_part, col_part)
    return tuple(
        x.reshape(OWN, OT, NC, NO).transpose(0, 2, 1, 3) for x in (row_res, col_res)
    )


def solution(mesh):
    placed = (
        P("aa", "ba", None, None),
        P(("aa", "ba"), None, None, None),
        P(("ba", "aa"), None, None, None),
        P(("aa", "ba"), None),
        P(("ba", "aa"), None),
        P(),
        P(),
        P(),
        P(),
    )
    return jax.shard_map(
        on_device,
        mesh=mesh,
        in_specs=placed,
        out_specs=(P(("aa", "ba"), None, None, None), P(("ba", "aa"), None, None, None)),
        check_vma=False,
    )
```

time: 571 us -> 61.2 us (0.11); the launches traced: 560 us -> 60 us
  waiting for transfers between devices: 269 us -> 0 us
  blocking collectives: 108 us -> 0 us
  matrix products: 82.4 us -> 0 us
  Pallas kernels: 0 us -> 52.5 us
  local copies, waits for them, and re-layouts: 53.6 us -> 6.79 us
  other arithmetic: 29.2 us -> 0 us
  between operations: 15.6 us -> 0.68 us
    unnamed x4 -> x0, waiting for transfers between devices: 269 us -> none
    all_gather x4 -> x0, blocking collectives: 108 us -> none  [the longest x1 38.8 us: on_device(): lax.all_gather(row_integral, 'ba', axis=0, tiled=True)]
    dot_general x160 -> x0, matrix products: 82.4 us -> none  [the longest x32 43.6 us: one_turn(): jnp.einsum('abil,ljk->abijk', pair_piece, table, preferred_element_type=j...]
    pallas_call x0 -> x3, Pallas kernels: none -> 52.5 us  [the longest x1 24.4 us: on_device(): pl.pallas_call(gather_body, out_shape=(whole, whole, jax.ShapeDtypeStruct...]
    reshape x2 -> x0, local copies, waits for them, and re-layouts: 16.7 us -> none  [the longest x1 16.6 us: on_device(): tail_table_whole.reshape(tail_count, all_occupied, tile_size, tile_size)]
    add x65 -> x0, other arithmetic: 15.8 us -> none  [the longest x32 13.1 us: one_turn(): lead_energy[:, None, None, None, None]]
    all_gather x2 -> x0, local copies, waits for them, and re-layouts: 14.2 us -> none  [the longest x1 10.7 us: on_device(): lax.all_gather(column_integral, 'aa', axis=0, tiled=True)]
    convert_element_type x32 -> x0, other arithmetic: 10.3 us -> none  [one_turn(): weighted = (triples / denominator).astype(jnp.bfloat16)]
  transfers between devices with their start and end apart: 2 -> 0, of which waited for: 2 -> 0; matrix products, arithmetic and copies ran while one was open for 1% -> 0% of each run, Pallas kernels for 0% -> 0%
where the time goes in v1:
time: 61.2 us; the launch traced here: 60 us
  Pallas kernels  52.5 us (86%)
  local copies, waits for them, and re-layouts  6.79 us (11%)
  between operations  0.68 us (1%)
    pallas_call x1, Pallas kernels, on_device(): pl.pallas_call(gather_body, out_shape=(whole, whole, jax.ShapeDtypeStruct...  24.4 us
    pallas_call x1, Pallas kernels, on_device(): pl.pallas_call(functools.partial(scatter_body, factor), out_shape=(part,...  15.7 us
    pallas_call x1, Pallas kernels, compute_call(): pl.pallas_call(compute_body, out_shape=(shape, shape), in_specs=[pl.Block...  12.3 us
    unnamed x18, local copies, waits for them, and re-layouts  6.79 us

profile of v1, /device:TPU:1, one launch (start us, length us, event | category | flops | bytes accessed | tf_op | source)
XLA Modules:
  0.0 60.0 jit_solution(10797765764596878238)
XLA Ops:
  0.6 0.0 copy-start
  0.6 0.7 %copy-done = bf16[4,3200]{1,0:T(4,128)(2,1)S(1)} copy-done((bf16[4,3200]{1,0:T(4,128)(2,1)S(1)}, bf16[4,3200]{1,0:T(4,128)(2,1)}, u32[]{:S(2)}) %copy-start) | copy-done | bytes 25624
  1.4 0.0 copy-start.1
  1.4 0.7 %copy-done.1 = bf16[4,3200]{1,0:T(4,128)(2,1)S(1)} copy-done((bf16[4,3200]{1,0:T(4,128)(2,1)S(1)}, bf16[4,3200]{1,0:T(4,128)(2,1)}, u32[]{:S(2)}) %copy-start.1) | copy-done | bytes 25624
  2.1 0.0 copy-start.2
  2.1 0.7 %copy-done.2 = bf16[2,3200]{1,0:T(2,128)(2,1)S(1)} copy-done((bf16[2,3200]{1,0:T(2,128)(2,1)S(1)}, bf16[2,3200]{1,0:T(2,128)(2,1)}, u32[]{:S(2)}) %copy-start.2) | copy-done | bytes 12824
  2.8 0.0 copy-start.3
  2.8 0.7 %copy-done.3 = bf16[4,2,5,128]{3,1,2,0:T(2,128)(2,1)S(1)} copy-done((bf16[4,2,5,128]{3,1,2,0:T(2,128)(2,1)S(1)}, bf16[4,2,5,128]{3,1,2,0:T(2,128)(2,1)}, u32[]{:S(2)}) %copy-start.3) | copy-done | bytes 10264
  3.5 0.0 copy-start.4
  3.5 0.7 %copy-done.4 = bf16[4,2,5,128]{3,1,2,0:T(2,128)(2,1)S(1)} copy-done((bf16[4,2,5,128]{3,1,2,0:T(2,128)(2,1)S(1)}, bf16[4,2,5,128]{3,1,2,0:T(2,128)(2,1)}, u32[]{:S(2)}) %copy-start.4) | copy-done | bytes 10264
  4.2 24.4 %shard_map.104 = (bf16[2304,128]{1,0:T(8,128)(2,1)S(1)}, bf16[2304,128]{1,0:T(8,128)(2,1)S(1)}, bf16[64,128]{1,0:T(8,128)(2,1)S(1)}) custom-call(bf16[4,3200]{1,0:T(4,128)(2,1)S(1)} %copy-done, bf16[4,3200]{1,0:T(4,128)(2,1)S(1)} %copy-done.1, bf16[2,3200]{1,0:T(2,128)(2,1)S(1)} %copy-done.2, bf16[40,128]{1,0:T(8,128)(2,1)S(1)} %bitcast.16, ...), custom_call_target="tpu_custom_call" | custom-call | tf_op jit(solution)/shard_map/pallas_call | solution.py:401
  28.7 0.0 copy-start.5
  28.7 0.7 %copy-done.5 = f32[1024]{0:T(1024)S(1)} copy-done((f32[1024]{0:T(1024)S(1)}, f32[1024]{0:T(1024)}, u32[]{:S(2)}) %copy-start.5) | copy-done | bytes 4120
  29.4 0.0 copy-start.6
  29.4 0.7 %copy-done.6 = f32[5]{0:T(128)S(1)} copy-done((f32[5]{0:T(128)S(1)}, f32[5]{0:T(128)}, u32[]{:S(2)}) %copy-start.6) | copy-done | bytes 44
  30.0 0.0 copy-start.7
  30.0 0.7 %copy-done.7 = f32[2]{0:T(128)S(1)} copy-done((f32[2]{0:T(128)S(1)}, f32[2]{0:T(128)}, u32[]{:S(2)}) %copy-start.7) | copy-done | bytes 32
  30.7 12.3 %shard_map.105 = (f32[640,128]{1,0:T(8,128)S(1)}, f32[640,128]{1,0:T(8,128)S(1)}) custom-call(bf16[64,5,64,128]{3,2,1,0:T(8,128)(2,1)} %bitcast.19, bf16[64,128]{1,0:T(8,128)(2,1)S(1)} %get-tuple-element.9.q_ref, bf16[2304,128]{1,0:T(8,128)(2,1)S(1)} %get-tuple-element.10.rows_ref, bf16[2304,128]{1,0:T(8,128)(2,1)S(1)} %get-tuple-element.11.cols_ref, ...), custom_call_target="tpu_custom_call" | custom-call | tf_op jit(solution)/shard_map/pallas_call | solution.py:311
  43.0 15.7 %shard_map.106 = (f32[40,128]{1,0:T(8,128)S(1)}, f32[40,128]{1,0:T(8,128)S(1)}) custom-call(f32[640,128]{1,0:T(8,128)S(1)} %get-tuple-element.12.row_ref, f32[640,128]{1,0:T(8,128)S(1)} %get-tuple-element.13.col_ref), custom_call_target="tpu_custom_call" | custom-call | tf_op jit(solution)/shard_map/pallas_call | solution.py:423
  58.7 0.6 %copy.13 = f32[4,2,5,128]{3,1,2,0:T(2,128)} copy(f32[4,2,5,128]{3,1,2,0:T(2,128)S(1)} %bitcast.15) | data formatting | bytes 40960
  59.4 0.6 %copy.14 = f32[4,2,5,128]{3,1,2,0:T(2,128)} copy(f32[4,2,5,128]{3,1,2,0:T(2,128)S(1)} %bitcast.14) | data formatting | bytes 40960
Async XLA Ops:
  0.6 0.7 %copy-start = (bf16[4,3200]{1,0:T(4,128)(2,1)S(1)}, bf16[4,3200]{1,0:T(4,128)(2,1)}, u32[]{:S(2)}) copy-start(bf16[4,3200]{1,0:T(4,128)(2,1)} %g_ref.1) | copy-start | bytes 76804
  1.4 0.7 %copy-start.1 = (bf16[4,3200]{1,0:T(4,128)(2,1)S(1)}, bf16[4,3200]{1,0:T(4,128)(2,1)}, u32[]{:S(2)}) copy-start(bf16[4,3200]{1,0:T(4,128)(2,1)} %h_ref.1) | copy-start | bytes 76804
  2.1 0.7 %copy-start.2 = (bf16[2,3200]{1,0:T(2,128)(2,1)S(1)}, bf16[2,3200]{1,0:T(2,128)(2,1)}, u32[]{:S(2)}) copy-start(bf16[2,3200]{1,0:T(2,128)(2,1)} %q_ref.1) | copy-start | bytes 38404
  2.8 0.7 %copy-start.3 = (bf16[4,2,5,128]{3,1,2,0:T(2,128)(2,1)S(1)}, bf16[4,2,5,128]{3,1,2,0:T(2,128)(2,1)}, u32[]{:S(2)}) copy-start(bf16[4,2,5,128]{3,1,2,0:T(2,128)(2,1)} %param.10) | copy-start | bytes 30724
  3.5 0.7 %copy-start.4 = (bf16[4,2,5,128]{3,1,2,0:T(2,128)(2,1)S(1)}, bf16[4,2,5,128]{3,1,2,0:T(2,128)(2,1)}, u32[]{:S(2)}) copy-start(bf16[4,2,5,128]{3,1,2,0:T(2,128)(2,1)} %param.11) | copy-start | bytes 30724
  28.7 0.7 %copy-start.5 = (f32[1024]{0:T(1024)S(1)}, f32[1024]{0:T(1024)}, u32[]{:S(2)}) copy-start(f32[1024]{0:T(1024)} %param.15) | copy-start | bytes 12292
  29.4 0.7 %copy-start.6 = (f32[5]{0:T(128)S(1)}, f32[5]{0:T(128)}, u32[]{:S(2)}) copy-start(f32[5]{0:T(128)} %oe_ref.1) | copy-start | bytes 64
  30.0 0.7 %copy-start.7 = (f32[2]{0:T(128)S(1)}, f32[2]{0:T(128)}, u32[]{:S(2)}) copy-start(f32[2]{0:T(128)} %se_ref.1) | copy-start | bytes 28

commit v2 on v0

v2 whole, which is shorter than its diff:
```python
import functools
import math

import jax
import jax.numpy as jnp
from jax import lax
from jax.experimental import pallas as pl
from jax.experimental.pallas import tpu as pltpu
from jax.sharding import PartitionSpec as P

F32 = jnp.float32
BF16 = jnp.bfloat16
MESH = pl.DeviceIdType.MESH
GROUP = 16
OWN = 4
OT = 5
JK = OT * OT
NC = 2
SI = OT * NC
NO = 128
CHUNK = 144
PART = 24
USED = OWN * OT
AROWS = 56
NT = (((1,), (1,)), ((), ()))


def dot_nt(x, y):
    return lax.dot_general(x, y, NT, preferred_element_type=F32)


def split_l(g_ref, h_ref, q_ref, r_ref, u_ref, row_chunk, col_chunk, q_out, amp):
    top = jnp.concatenate([g_ref[...].astype(F32), h_ref[...].astype(F32)], 0)
    low = jnp.concatenate(
        [q_ref[...].astype(F32), jnp.zeros((6, JK * NO), F32)], 0
    )
    row = lax.broadcasted_iota(jnp.int32, (NO, NO), 0)
    col = lax.broadcasted_iota(jnp.int32, (NO, NO), 1)
    perm = (row == ((JK * col) & 127)).astype(F32).astype(BF16)
    stacked = jnp.concatenate(
        [
            part[:, m * NO : (m + 1) * NO]
            for m in range(JK)
            for part in (top, low)
        ],
        0,
    ).astype(BF16)
    moved = jnp.dot(stacked, perm, preferred_element_type=F32)
    lane = lax.broadcasted_iota(jnp.int32, (8, NO), 1)
    tops, lows = [], []
    for jk in range(JK):
        source = (JK * ((lane - 41 * jk) & 127) + jk) >> 7
        t = moved[0:8]
        w = moved[8:16]
        for m in range(1, JK):
            mask = source == m
            t = jnp.where(mask, moved[16 * m : 16 * m + 8], t)
            w = jnp.where(mask, moved[16 * m + 8 : 16 * m + 16], w)
        shift = (-41 * jk) % 128
        if shift:
            t = pltpu.roll(t, shift, 1)
            w = pltpu.roll(w, shift, 1)
        tops.append(t)
        lows.append(w)
    for which, (src, dst) in enumerate(((r_ref, row_chunk), (u_ref, col_chunk))):
        amp[...] = src[...].astype(F32)
        pieces = [t[4 * which : 4 * which + 4] for t in tops]
        pieces += [
            amp[pl.ds(i * NC + s, OWN, stride=SI), :]
            for s in range(NC)
            for i in range(OT)
        ]
        pieces.append(jnp.zeros((4, NO), F32))
        for k in range(9):
            dst[16 * k : 16 * k + 16, :] = jnp.concatenate(
                pieces[4 * k : 4 * k + 4], 0
            ).astype(BF16)
    rows = [lows[jk][s : s + 1] for s in range(NC) for jk in range(JK)]
    rows.append(jnp.zeros((64 - NC * JK, NO), F32))
    q_out[...] = jnp.concatenate(rows, 0).astype(BF16)


class Place:
    def __init__(self):
        self.a = lax.axis_index("aa")
        self.b = lax.axis_index("ba")
        self.core = lax.rem(self.a, 2)
        self.y = lax.rem(self.a // 2, 4)
        self.xl = self.a // 8
        self.xh = self.b // 8
        self.z = lax.rem(self.b, 8)

    def index_b(self, q, k):
        xh = 1 - self.xh if q else self.xh
        return xh * 8 + lax.rem(self.z - k + 8, 8)

    def along_b(self, q, k):
        return (self.a, self.index_b(q, k))

    def index_a(self, q, d, c):
        xl = 1 - self.xl if q else self.xl
        core = 1 - self.core if c else self.core
        return (xl * 4 + lax.rem(self.y - d + 4, 4)) * 2 + core

    def along_a(self, q, d, c):
        return (self.index_a(q, d, c), self.b)


def compute_a(here, t_ref, q_ref, a_out, first, count):
    q = q_ref[0:AROWS, :]

    def pair(n, _):
        at_k = n // 2
        v = 2 * lax.rem(n, 2)
        zk = lax.rem(here.z - at_k + 8, 8)
        near = (here.xh * 8 + zk) * OWN + v
        far = ((1 - here.xh) * 8 + zk) * OWN + v
        for i in range(OT):
            block = jnp.concatenate(
                [t_ref[near, i], t_ref[far, i], t_ref[near + 1, i], t_ref[far + 1, i]], 0
            )
            part = dot_nt(q, block)
            for half in range(2):
                at = pl.multiple_of((2 * n + half) * (OT * AROWS) + i * AROWS, 8)
                a_out[pl.ds(at, AROWS), :] = part[:, half * NO : (half + 1) * NO]
        return 0

    lax.fori_loop(first, first + count, pair, 0)


def pair_energy(here, ve_ref):
    lane = lax.broadcasted_iota(jnp.int32, (32, NO), 1)
    row = lax.broadcasted_iota(jnp.int32, (32, NO), 0)
    zk = (here.z - (row >> 2)) & 7
    lead = jnp.broadcast_to(ve_ref[pl.ds(here.a // 2, 1), :], (32, NO))
    first = lax.rem(here.a, 2) * 64
    halves = []
    for xh in (here.xh, 1 - here.xh):
        at = first + (xh * 8 + zk) * OWN + (row & 3)
        halves.append(jnp.sum(jnp.where(lane == at, lead, 0.0), 1, keepdims=True))
    tail = ve_ref[pl.ds(here.b // 2, 1), :]
    turned = pltpu.roll(jnp.broadcast_to(tail, (8, NO)), 64, 1)[0:1]
    keep = (lane[0:1] // 64) == lax.rem(here.b, 2)
    tail = jnp.where(keep, tail, turned)
    return jnp.where(lane < 64, halves[0], halves[1]) + tail


def spread(src, wide):
    for k in range(9):
        blocks = [
            src[e * CHUNK + 16 * k : e * CHUNK + 16 * k + 16, :].astype(F32)
            for e in range(GROUP)
        ]
        for c in range(4):
            at = 4 * k + c
            if at >= JK + SI:
                continue
            tile = jnp.concatenate([b[4 * c : 4 * c + 4] for b in blocks], 0)
            wide(at, tile.astype(BF16))


def put_rows(g2, r2, at, tile):
    dst, c = (g2, at) if at < JK else (r2, at - JK)
    dst[c * 32 : c * 32 + 32, 0:NO] = tile[0:32]
    dst[c * 32 : c * 32 + 32, NO : 2 * NO] = tile[32:64]


def put_cols(bdh, bdu, at, tile):
    dst, c = (bdh, at) if at < JK else (bdu, at - JK)
    dst[c * NO : c * NO + 64, 0:NO] = tile
    dst[c * NO + 64 : c * NO + NO, NO : 2 * NO] = tile


def clear_off(bdh, bdu):
    zero = jnp.zeros((64, NO), BF16)
    for dst, count in ((bdh, JK), (bdu, SI)):
        for c in range(count):
            dst[c * NO : c * NO + 64, NO : 2 * NO] = zero
            dst[c * NO + 64 : c * NO + NO, 0:NO] = zero


def compute_pc(g2, r2, bdh, bdu, p_out, c_out):
    r = r2[...]

    for n in range(JK // 2 + 1):
        width = 2 if n < JK // 2 else 1
        part = dot_nt(r, bdh[2 * n * NO : (2 * n + width) * NO, :])
        for half in range(width):
            p_out[(2 * n + half) * 320 : (2 * n + half + 1) * 320, :] = part[
                :, half * NO : (half + 1) * NO
            ]
    for n in range(OT):
        for m in range(5):
            part = dot_nt(
                g2[m * 160 : (m + 1) * 160, :], bdu[2 * n * NO : (2 * n + 2) * NO, :]
            )
            for half in range(2):
                at = (2 * n + half) * 800 + m * 160
                c_out[at : at + 160, :] = part[:, half * NO : (half + 1) * NO]


def weigh(oe_ref, se_ref, base, s, a_in, p_in, c_in, yr, yc):
    start = base + se_ref[s]

    def one(i, _):
        for j in range(OT):
            for k in range(OT):
                jk = j * OT + k
                ki = k * OT + i
                ij = i * OT + j
                energy = (oe_ref[i] + oe_ref[j]) + oe_ref[k]
                tiles = []
                for v in range(4):
                    first = v * 8 * OT * AROWS + s * JK
                    w = a_in[pl.ds(first + i * AROWS + jk, 8, stride=OT * AROWS), :]
                    w = w + a_in[pl.ds(first + j * AROWS + ki, 8, stride=OT * AROWS), :]
                    at = pl.multiple_of(jk * 320 + (s * OT + i) * 32 + v * 8, 8)
                    w = w + p_in[pl.ds(at, 8), :]
                    at = pl.multiple_of(ij * 320 + (s * OT + k) * 32 + v * 8, 8)
                    w = w + p_in[pl.ds(at, 8), :]
                    at = pl.multiple_of((s * OT + j) * 800 + ki * 32 + v * 8, 8)
                    w = w + c_in[pl.ds(at, 8), :]
                    at = pl.multiple_of((s * OT + k) * 800 + ij * 32 + v * 8, 8)
                    w = w + c_in[pl.ds(at, 8), :]
                    tiles.append(w / (start[v * 8 : v * 8 + 8] - energy))
                y = jnp.concatenate(tiles, 0).astype(BF16)
                at = pl.multiple_of((s * OT + i) * 32, 32)
                yr[pl.ds(at, 32), jk * NO : (jk + 1) * NO] = y
                at = pl.multiple_of((s * OT + j) * 800 + ki * 32, 32)
                yc[pl.ds(at, 32), :] = y
        return 0

    lax.fori_loop(0, OT, one, 0)


def deal(res, out):
    for i in range(OT):
        for v in range(OWN):
            out[pl.ds(v * OT + i, GROUP, stride=PART), :] = res[
                pl.ds(i * 64 + v, GROUP, stride=OWN), :
            ]


def row_residual(s, bdh, yr, res, row_out):
    out = jnp.dot(yr[s * 160 : (s + 1) * 160, :], bdh[...], preferred_element_type=F32)
    for i in range(OT):
        for half in range(2):
            res[i * 64 + half * 32 : i * 64 + half * 32 + 32, :] = out[
                i * 32 : i * 32 + 32, half * NO : (half + 1) * NO
            ]
    deal(res, row_out)


def col_residual(s, turned, yc, res, col_out):
    lane = lax.broadcasted_iota(jnp.int32, (NO, NO), 1)
    wide = jnp.concatenate(
        [yc[(s * OT + j) * 800 : (s * OT + j + 1) * 800, :] for j in range(OT)], 1
    )
    out = jnp.dot(turned[...], wide, preferred_element_type=F32)
    for j in range(OT):
        piece = out[:, j * NO : (j + 1) * NO]
        both = jnp.where(lane < 64, piece[0:NO], piece[NO:]).T
        res[j * 64 : j * 64 + 64, :] = both[0:64] + both[64:128]
    deal(res, col_out)


class Gather:
    def __init__(self, here, rows, cols, send_sems, row_sems, col_sems):
        self.here, self.rows, self.cols = here, rows, cols
        self.send_sems, self.row_sems, self.col_sems = send_sems, row_sems, col_sems
        self.sent = []

    def copy(self, src, dst, recv_sem, target):
        copy = pltpu.make_async_remote_copy(
            src_ref=src,
            dst_ref=dst,
            send_sem=self.send_sems.at[len(self.sent)],
            recv_sem=recv_sem,
            device_id=target,
            device_id_type=MESH,
        )
        copy.start()
        self.sent.append(copy)

    def row_slot(self, q, k):
        at = (q * 8 + k) * CHUNK
        return self.rows.at[at : at + CHUNK, :]

    def col_slot(self, q, d, c):
        at = pl.multiple_of(self.here.index_a(q, d, c) * CHUNK, 16)
        return self.cols.at[pl.ds(at, CHUNK), :]

    def swap_row(self):
        self.copy(
            self.row_slot(0, 0), self.row_slot(1, 0), self.row_sems.at[1, 0],
            self.here.along_b(1, 0),
        )

    def up(self, q, k):
        self.copy(
            self.row_slot(q, k), self.row_slot(q, k + 1), self.row_sems.at[q, k + 1],
            self.here.along_b(0, -1),
        )

    def down(self, q, k):
        to = (k + 7) % 8
        self.copy(
            self.row_slot(q, k), self.row_slot(q, to), self.row_sems.at[q, to],
            self.here.along_b(0, 1),
        )

    def got_row(self, q, k):
        pltpu.make_async_remote_copy(
            src_ref=self.row_slot(q, k), dst_ref=self.row_slot(q, k),
            send_sem=self.row_sems.at[q, k], recv_sem=self.row_sems.at[q, k],
            device_id=self.here.along_b(0, 1), device_id_type=MESH,
        ).wait_recv()

    def col_to(self, q, d, c, kind, step, target):
        slot = self.col_slot(q, d, c)
        self.copy(slot, slot, self.col_sems.at[kind, step], target)

    def swap_col(self):
        self.col_to(0, 0, 0, 1, 0, self.here.along_a(1, 0, 0))

    def round_col(self, q):
        for d in range(1, 4):
            self.col_to(q, 0, 0, q, d, self.here.along_a(0, -d, 0))

    def twin_col(self, q, d):
        self.col_to(q, d, 0, 2 + q, d, self.here.along_a(0, 0, 1))

    def got_col(self, kind, d):
        slot = self.col_slot(kind % 2, d, kind // 2)
        pltpu.make_async_remote_copy(
            src_ref=slot, dst_ref=slot,
            send_sem=self.col_sems.at[kind, d], recv_sem=self.col_sems.at[kind, d],
            device_id=self.here.along_b(0, 1), device_id_type=MESH,
        ).wait_recv()


def scatter(here, s, along_rows, part, into, send_sems, recv_sems):
    copies = []
    for n in range(1, GROUP):
        if along_rows:
            target = here.along_b(n // 8, n % 8)
            at = n * PART
        else:
            target = here.along_a(n // 8, n // 2 % 4, n % 2)
            at = pl.multiple_of(target[0] * PART, 8)
        copy = pltpu.make_async_remote_copy(
            src_ref=part.at[s, pl.ds(at, PART), :],
            dst_ref=into.at[s, n * PART : (n + 1) * PART, :],
            send_sem=send_sems.at[s, n],
            recv_sem=recv_sems.at[s, n],
            device_id=target,
            device_id_type=MESH,
        )
        copy.start()
        copies.append(copy)
    return copies


def whole_body(
    factor,
    t_hbm, g_hbm, h_hbm, q_hbm, r_hbm, u_hbm, ve_hbm, oe_hbm, se_hbm,
    row_out, col_out,
    t_ref, g_in, h_in, q_in, r_in, u_in, ve_ref, oe_ref, se_ref,
    q_ref, amp, rows, cols, a_ref, g2, r2, bdh, bdu, p_ref, c_ref, yr, yc, turned, res,
    row_part, col_part, row_into, col_into, last,
    in_sems, gather_sems, row_sems, col_sems, out_row_sems, out_col_sems, sum_row_sems,
    sum_col_sems,
):
    here = Place()
    loads = [
        pltpu.make_async_copy(src, dst, in_sems.at[n])
        for n, (src, dst) in enumerate(
            (
                (g_hbm, g_in), (h_hbm, h_in), (q_hbm, q_in), (r_hbm, r_in), (u_hbm, u_in),
                (ve_hbm, ve_ref), (oe_hbm, oe_ref), (se_hbm, se_ref), (t_hbm, t_ref),
            )
        )
    ]
    for load in loads:
        load.start()
    barrier = pltpu.get_barrier_semaphore()
    near = [here.along_b(0, 1), here.along_b(0, 7), here.along_b(1, 0)]
    near += [here.along_a(0, d, 0) for d in range(1, 4)]
    near += [here.along_a(1, 0, 0), here.along_a(0, 0, 1)]
    for target in near:
        pl.semaphore_signal(barrier, inc=1, device_id=target, device_id_type=MESH)
    for load in loads[:5]:
        load.wait()
    own_col = cols.at[pl.ds(pl.multiple_of(here.a * CHUNK, 16), CHUNK), :]
    split_l(
        g_in, h_in, q_in, r_in, u_in, rows.at[0:CHUNK, :], own_col, q_ref, amp
    )
    pl.semaphore_wait(barrier, len(near))
    net = Gather(here, rows, cols, gather_sems, row_sems, col_sems)
    net.swap_row()
    net.up(0, 0)
    net.down(0, 0)
    net.swap_col()
    net.round_col(0)
    net.twin_col(0, 0)
    clear_off(bdh, bdu)
    for load in loads[5:]:
        load.wait()
    compute_a(here, t_ref, q_ref, a_ref, 0, 2)
    net.got_row(0, 1)
    net.up(0, 1)
    net.got_row(0, 7)
    net.down(0, 7)
    net.got_row(1, 0)
    net.up(1, 0)
    net.down(1, 0)
    net.got_col(1, 0)
    net.round_col(1)
    net.twin_col(1, 0)
    compute_a(here, t_ref, q_ref, a_ref, 2, 3)
    net.got_row(0, 2)
    net.up(0, 2)
    net.got_row(0, 6)
    net.down(0, 6)
    for d in range(1, 4):
        net.got_col(0, d)
        net.twin_col(0, d)
    compute_a(here, t_ref, q_ref, a_ref, 5, 3)
    net.got_row(1, 1)
    net.up(1, 1)
    net.got_row(1, 7)
    net.down(1, 7)
    for d in range(1, 4):
        net.got_col(1, d)
        net.twin_col(1, d)
    compute_a(here, t_ref, q_ref, a_ref, 8, 3)
    net.got_row(0, 3)
    net.up(0, 3)
    net.got_row(0, 5)
    compute_a(here, t_ref, q_ref, a_ref, 11, 3)
    net.got_row(1, 2)
    net.up(1, 2)
    net.got_row(1, 6)
    net.down(1, 6)
    compute_a(here, t_ref, q_ref, a_ref, 14, 2)
    net.got_row(1, 3)
    net.got_row(1, 5)
    net.down(1, 5)
    for kind in (2, 3):
        for d in range(4):
            net.got_col(kind, d)
    spread(cols, functools.partial(put_cols, bdh, bdu))
    base = pair_energy(here, ve_ref)
    net.got_row(0, 4)
    net.got_row(1, 4)
    spread(rows, functools.partial(put_rows, g2, r2))
    for copy in net.sent:
        copy.wait_send()
    compute_pc(g2, r2, bdh, bdu, p_ref, c_ref)
    turned[...] = g2[...].T
    sums = [[], []]
    for s in range(NC):
        weigh(oe_ref, se_ref, base, s, a_ref, p_ref, c_ref, yr, yc)
        row_residual(s, bdh, yr, res, row_part.at[s])
        sums[0] += scatter(here, s, True, row_part, row_into, out_row_sems, sum_row_sems)
    for s in range(NC):
        col_residual(s, turned, yc, res, col_part.at[s])
        sums[1] += scatter(here, s, False, col_part, col_into, out_col_sems, sum_col_sems)
    for which, (part, into, out, own) in enumerate(
        (
            (col_part, col_into, col_out, pl.multiple_of(here.a * PART, 8)),
            (row_part, row_into, row_out, 0),
        )
    ):
        for s in range(NC):
            total = part[s, pl.ds(own, PART), :]
            for n in range(1, GROUP):
                sums[1 - which][s * (GROUP - 1) + n - 1].wait_recv()
                total = total + into[s, n * PART : (n + 1) * PART, :]
            last[pl.ds(s, PART, stride=NC), :] = total * factor
        out[...] = last[0 : NC * USED, :]
    for copy in sums[0] + sums[1]:
        copy.wait_send()


def on_device(
    pair_amplitude,
    row_amplitude,
    column_amplitude,
    row_integral,
    column_integral,
    step_integral,
    virtual_energy,
    occupied_energy,
    step_energy,
):
    factor = 1.0 / (math.sqrt(virtual_energy.shape[0]) * OT)
    t = pair_amplitude.transpose(0, 2, 1, 3)
    r = row_amplitude.transpose(0, 2, 1, 3).reshape(OWN * SI, NO)
    u = column_amplitude.transpose(0, 2, 1, 3).reshape(OWN * SI, NO)
    ve = virtual_energy.reshape(8, NO)
    operands = (
        t, row_integral, column_integral, step_integral, r, u, ve, occupied_energy, step_energy
    )
    out = jax.ShapeDtypeStruct((NC * USED, NO), F32)
    vm = pl.BlockSpec(memory_space=pltpu.VMEM)
    spaces = [pltpu.VMEM] * 7 + [pltpu.SMEM] * 2
    order = (0, 1, 2, 3, 4, 5, 6, 7, 8)
    dma = pltpu.SemaphoreType.DMA
    results = pl.pallas_call(
        functools.partial(whole_body, factor),
        out_shape=(out, out),
        in_specs=[pl.BlockSpec(memory_space=pl.ANY)] * 9,
        out_specs=(vm, vm),
        scratch_shapes=[spaces[n](operands[n].shape, operands[n].dtype) for n in order]
        + [
            pltpu.VMEM((64, NO), BF16),
            pltpu.VMEM((OWN * SI, NO), F32),
            pltpu.VMEM((GROUP * CHUNK, NO), BF16),
            pltpu.VMEM((GROUP * CHUNK, NO), BF16),
            pltpu.VMEM((32 * OT * AROWS, NO), F32),
            pltpu.VMEM((JK * 32, 2 * NO), BF16),
            pltpu.VMEM((SI * 32, 2 * NO), BF16),
            pltpu.VMEM((JK * NO, 2 * NO), BF16),
            pltpu.VMEM((SI * NO, 2 * NO), BF16),
            pltpu.VMEM((JK * 320, NO), F32),
            pltpu.VMEM((SI * 800, NO), F32),
            pltpu.VMEM((320, JK * NO), BF16),
            pltpu.VMEM((SI * 800, NO), BF16),
            pltpu.VMEM((2 * NO, 800), BF16),
            pltpu.VMEM((OT * 64, NO), F32),
            pltpu.VMEM((NC, GROUP * PART, NO), F32),
            pltpu.VMEM((NC, GROUP * PART, NO), F32),
            pltpu.VMEM((NC, GROUP * PART, NO), F32),
            pltpu.VMEM((NC, GROUP * PART, NO), F32),
            pltpu.VMEM((NC * PART, NO), F32),
            dma((9,)),
            dma((30,)),
            dma((2, 8)),
            dma((4, 4)),
            dma((NC, GROUP)),
            dma((NC, GROUP)),
            dma((NC, GROUP)),
            dma((NC, GROUP)),
        ],
        compiler_params=pltpu.CompilerParams(
            collective_id=0, has_side_effects=True, vmem_limit_bytes=56 * 2**20
        ),
    )(*operands)
    return tuple(
        x.reshape(OWN, OT, NC, NO).transpose(0, 2, 1, 3) for x in results
    )


def solution(mesh):
    placed = (
        P("aa", "ba", None, None),
        P(("aa", "ba"), None, None, None),
        P(("ba", "aa"), None, None, None),
        P(("aa", "ba"), None),
        P(("ba", "aa"), None),
        P(),
        P(),
        P(),
        P(),
    )
    return jax.shard_map(
        on_device,
        mesh=mesh,
        in_specs=placed,
        out_specs=(P(("aa", "ba"), None, None, None), P(("ba", "aa"), None, None, None)),
        check_vma=False,
    )
```

time: 571 us -> 46.7 us (0.08); the launches traced: 560 us -> 46.5 us
  waiting for transfers between devices: 269 us -> 0 us
  blocking collectives: 108 us -> 0 us
  matrix products: 82.4 us -> 0 us
  local copies, waits for them, and re-layouts: 53.6 us -> 2.67 us
  Pallas kernels: 0 us -> 43.2 us
  other arithmetic: 29.2 us -> 0 us
  between operations: 15.6 us -> 0.64 us
    unnamed x4 -> x0, waiting for transfers between devices: 269 us -> none
    all_gather x4 -> x0, blocking collectives: 108 us -> none  [the longest x1 38.8 us: on_device(): lax.all_gather(row_integral, 'ba', axis=0, tiled=True)]
    dot_general x160 -> x0, matrix products: 82.4 us -> none  [the longest x32 43.6 us: one_turn(): jnp.einsum('abil,ljk->abijk', pair_piece, table, preferred_element_type=j...]
    pallas_call x0 -> x1, Pallas kernels: none -> 43.2 us  [on_device(): pl.pallas_call(functools.partial(whole_body, factor), out_shape=(out, out...]
    reshape x2 -> x0, local copies, waits for them, and re-layouts: 16.7 us -> none  [the longest x1 16.6 us: on_device(): tail_table_whole.reshape(tail_count, all_occupied, tile_size, tile_size)]
    add x65 -> x0, other arithmetic: 15.8 us -> none  [the longest x32 13.1 us: one_turn(): lead_energy[:, None, None, None, None]]
    all_gather x2 -> x0, local copies, waits for them, and re-layouts: 14.2 us -> none  [the longest x1 10.7 us: on_device(): lax.all_gather(column_integral, 'aa', axis=0, tiled=True)]
    convert_element_type x32 -> x0, other arithmetic: 10.3 us -> none  [one_turn(): weighted = (triples / denominator).astype(jnp.bfloat16)]
  transfers between devices with their start and end apart: 2 -> 0, of which waited for: 2 -> 0; matrix products, arithmetic and copies ran while one was open for 1% -> 0% of each run, Pallas kernels for 0% -> 0%
where the time goes in v2:
time: 46.7 us; the launch traced here: 46.5 us
  Pallas kernels  43.2 us (93%)
  local copies, waits for them, and re-layouts  2.67 us (6%)
  between operations  0.64 us (1%)
    pallas_call x1, Pallas kernels, on_device(): pl.pallas_call(functools.partial(whole_body, factor), out_shape=(out, out...  43.2 us
    unnamed x2, local copies, waits for them, and re-layouts  2.67 us

profile of v2, /device:TPU:1, one launch (start us, length us, event | category | flops | bytes accessed | tf_op | source)
XLA Modules:
  0.0 46.5 jit_solution(5656387871798986174)
XLA Ops:
  0.6 43.2 %shard_map.104 = (f32[40,128]{1,0:T(8,128)}, f32[40,128]{1,0:T(8,128)}) custom-call(bf16[64,5,64,128]{3,2,1,0:T(8,128)(2,1)} %bitcast.14, bf16[4,3200]{1,0:T(4,128)(2,1)} %g_hbm.1, bf16[4,3200]{1,0:T(4,128)(2,1)} %h_hbm.1, bf16[2,3200]{1,0:T(2,128)(2,1)} %q_hbm.1, bf16[40,128]{1,0:T(8,128)(2,1)} %bitcast.17, bf16[40,128]{1,0:T(8,128)(2,1)} %bitcast.18, ...), custom_call_target="tpu_custom_call" | custom-call | tf_op jit(solution)/shard_map/pallas_call | solution.py:510
  43.8 1.3 %copy.13 = f32[4,2,5,128]{3,1,2,0:T(2,128)} copy(f32[4,2,5,128]{3,1,2,0:T(2,128)} %bitcast.16) | data formatting | bytes 40960
  45.1 1.3 %copy.14 = f32[4,2,5,128]{3,1,2,0:T(2,128)} copy(f32[4,2,5,128]{3,1,2,0:T(2,128)} %bitcast.15) | data formatting | bytes 40960

commit v3 on v2

--- a/solution.py
+++ b/solution.py
@@ -21,6 +21,7 @@
 CHUNK = 144
 PART = 24
 USED = OWN * OT
+ORDER = (1, 7, 2, 6, 3, 5, 4)
 AROWS = 56
 NT = (((1,), (1,)), ((), ()))
 
@@ -29,55 +30,55 @@
     return lax.dot_general(x, y, NT, preferred_element_type=F32)
 
 
-def split_l(g_ref, h_ref, q_ref, r_ref, u_ref, row_chunk, col_chunk, q_out, amp):
-    top = jnp.concatenate([g_ref[...].astype(F32), h_ref[...].astype(F32)], 0)
-    low = jnp.concatenate(
-        [q_ref[...].astype(F32), jnp.zeros((6, JK * NO), F32)], 0
-    )
+def by_jk(moved, first, stride, count):
+    lane = lax.broadcasted_iota(jnp.int32, (8, NO), 1)
+    found = []
+    for jk in range(JK):
+        source = (JK * ((lane - 41 * jk) & 127) + jk) >> 7
+        t = moved[first : first + 8]
+        for m in range(1, JK):
+            at = first + stride * m
+            t = jnp.where(source == m, moved[at : at + 8], t)
+        shift = (-41 * jk) % 128
+        found.append(pltpu.roll(t, shift, 1) if shift else t)
+    return found
+
+
+def permute_lanes(parts):
     row = lax.broadcasted_iota(jnp.int32, (NO, NO), 0)
     col = lax.broadcasted_iota(jnp.int32, (NO, NO), 1)
     perm = (row == ((JK * col) & 127)).astype(F32).astype(BF16)
     stacked = jnp.concatenate(
-        [
-            part[:, m * NO : (m + 1) * NO]
-            for m in range(JK)
-            for part in (top, low)
-        ],
-        0,
+        [part[:, m * NO : (m + 1) * NO] for m in range(JK) for part in parts], 0
     ).astype(BF16)
-    moved = jnp.dot(stacked, perm, preferred_element_type=F32)
-    lane = lax.broadcasted_iota(jnp.int32, (8, NO), 1)
-    tops, lows = [], []
-    for jk in range(JK):
-        source = (JK * ((lane - 41 * jk) & 127) + jk) >> 7
-        t = moved[0:8]
-        w = moved[8:16]
-        for m in range(1, JK):
-            mask = source == m
-            t = jnp.where(mask, moved[16 * m : 16 * m + 8], t)
-            w = jnp.where(mask, moved[16 * m + 8 : 16 * m + 16], w)
-        shift = (-41 * jk) % 128
-        if shift:
-            t = pltpu.roll(t, shift, 1)
-            w = pltpu.roll(w, shift, 1)
-        tops.append(t)
-        lows.append(w)
-    for which, (src, dst) in enumerate(((r_ref, row_chunk), (u_ref, col_chunk))):
-        amp[...] = src[...].astype(F32)
-        pieces = [t[4 * which : 4 * which + 4] for t in tops]
-        pieces += [
-            amp[pl.ds(i * NC + s, OWN, stride=SI), :]
-            for s in range(NC)
-            for i in range(OT)
-        ]
-        pieces.append(jnp.zeros((4, NO), F32))
-        for k in range(9):
-            dst[16 * k : 16 * k + 16, :] = jnp.concatenate(
-                pieces[4 * k : 4 * k + 4], 0
-            ).astype(BF16)
+    return jnp.dot(stacked, perm, preferred_element_type=F32)
+
+
+def put_chunk(tables, src, amp, dst):
+    amp[...] = src[...].astype(F32)
+    pieces = tables + [
+        amp[pl.ds(i * NC + s, OWN, stride=SI), :] for s in range(NC) for i in range(OT)
+    ]
+    pieces.append(jnp.zeros((4, NO), F32))
+    for k in range(9):
+        dst[16 * k : 16 * k + 16, :] = jnp.concatenate(
+            pieces[4 * k : 4 * k + 4], 0
+        ).astype(BF16)
+
+
+def split_q(q_ref, q_out):
+    low = jnp.concatenate([q_ref[...].astype(F32), jnp.zeros((6, JK * NO), F32)], 0)
+    lows = by_jk(permute_lanes([low]), 0, 8, JK)
     rows = [lows[jk][s : s + 1] for s in range(NC) for jk in range(JK)]
     rows.append(jnp.zeros((64 - NC * JK, NO), F32))
     q_out[...] = jnp.concatenate(rows, 0).astype(BF16)
+
+
+def split_l(g_ref, h_ref, r_ref, u_ref, row_chunk, col_chunk, amp):
+    top = jnp.concatenate([g_ref[...].astype(F32), h_ref[...].astype(F32)], 0)
+    tops = by_jk(permute_lanes([top]), 0, 8, JK)
+    put_chunk([t[0:4] for t in tops], r_ref, amp.at[0], row_chunk)
+    put_chunk([t[4:8] for t in tops], u_ref, amp.at[1], col_chunk)
 
 
 class Place:
@@ -233,35 +234,37 @@
     lax.fori_loop(0, OT, one, 0)
 
 
-def deal(res, out):
+def deal(res, wide, out):
     for i in range(OT):
         for v in range(OWN):
-            out[pl.ds(v * OT + i, GROUP, stride=PART), :] = res[
+            wide[pl.ds(v * OT + i, GROUP, stride=PART), :] = res[
                 pl.ds(i * 64 + v, GROUP, stride=OWN), :
             ]
-
-
-def row_residual(s, bdh, yr, res, row_out):
+    for n in range(GROUP):
+        out[n] = wide[n * PART : n * PART + USED, :]
+
+
+def row_residual(s, bdh, yr, res, wide, row_out):
     out = jnp.dot(yr[s * 160 : (s + 1) * 160, :], bdh[...], preferred_element_type=F32)
     for i in range(OT):
         for half in range(2):
             res[i * 64 + half * 32 : i * 64 + half * 32 + 32, :] = out[
                 i * 32 : i * 32 + 32, half * NO : (half + 1) * NO
             ]
-    deal(res, row_out)
-
-
-def col_residual(s, turned, yc, res, col_out):
+    deal(res, wide, row_out)
+
+
+def col_residual(s, turned, yc, res, wide, col_out):
     lane = lax.broadcasted_iota(jnp.int32, (NO, NO), 1)
-    wide = jnp.concatenate(
+    moved = jnp.concatenate(
         [yc[(s * OT + j) * 800 : (s * OT + j + 1) * 800, :] for j in range(OT)], 1
     )
-    out = jnp.dot(turned[...], wide, preferred_element_type=F32)
+    out = jnp.dot(turned[...], moved, preferred_element_type=F32)
     for j in range(OT):
         piece = out[:, j * NO : (j + 1) * NO]
         both = jnp.where(lane < 64, piece[0:NO], piece[NO:]).T
         res[j * 64 : j * 64 + 64, :] = both[0:64] + both[64:128]
-    deal(res, col_out)
+    deal(res, wide, col_out)
 
 
 class Gather:
@@ -290,23 +293,16 @@
         at = pl.multiple_of(self.here.index_a(q, d, c) * CHUNK, 16)
         return self.cols.at[pl.ds(at, CHUNK), :]
 
-    def swap_row(self):
+    def along_z(self, k):
         self.copy(
-            self.row_slot(0, 0), self.row_slot(1, 0), self.row_sems.at[1, 0],
+            self.row_slot(0, 0), self.row_slot(0, k), self.row_sems.at[0, k],
+            self.here.along_b(0, -k),
+        )
+
+    def across_x(self, k):
+        self.copy(
+            self.row_slot(0, k), self.row_slot(1, k), self.row_sems.at[1, k],
             self.here.along_b(1, 0),
-        )
-
-    def up(self, q, k):
-        self.copy(
-            self.row_slot(q, k), self.row_slot(q, k + 1), self.row_sems.at[q, k + 1],
-            self.here.along_b(0, -1),
-        )
-
-    def down(self, q, k):
-        to = (k + 7) % 8
-        self.copy(
-            self.row_slot(q, k), self.row_slot(q, to), self.row_sems.at[q, to],
-            self.here.along_b(0, 1),
         )
 
     def got_row(self, q, k):
@@ -344,13 +340,13 @@
     for n in range(1, GROUP):
         if along_rows:
             target = here.along_b(n // 8, n % 8)
-            at = n * PART
+            at = n
         else:
             target = here.along_a(n // 8, n // 2 % 4, n % 2)
-            at = pl.multiple_of(target[0] * PART, 8)
+            at = target[0]
         copy = pltpu.make_async_remote_copy(
-            src_ref=part.at[s, pl.ds(at, PART), :],
-            dst_ref=into.at[s, n * PART : (n + 1) * PART, :],
+            src_ref=part.at[s, at],
+            dst_ref=into.at[s, n],
             send_sem=send_sems.at[s, n],
             recv_sem=recv_sems.at[s, n],
             device_id=target,
@@ -362,11 +358,10 @@
 
 
 def whole_body(
-    factor,
     t_hbm, g_hbm, h_hbm, q_hbm, r_hbm, u_hbm, ve_hbm, oe_hbm, se_hbm,
     row_out, col_out,
     t_ref, g_in, h_in, q_in, r_in, u_in, ve_ref, oe_ref, se_ref,
-    q_ref, amp, rows, cols, a_ref, g2, r2, bdh, bdu, p_ref, c_ref, yr, yc, turned, res,
+    q_ref, amp, rows, cols, a_ref, g2, r2, bdh, bdu, p_ref, c_ref, yr, yc, turned, res, wide,
     row_part, col_part, row_into, col_into, last,
     in_sems, gather_sems, row_sems, col_sems, out_row_sems, out_col_sems, sum_row_sems,
     sum_col_sems,
@@ -376,7 +371,7 @@
         pltpu.make_async_copy(src, dst, in_sems.at[n])
         for n, (src, dst) in enumerate(
             (
-                (g_hbm, g_in), (h_hbm, h_in), (q_hbm, q_in), (r_hbm, r_in), (u_hbm, u_in),
+                (g_hbm, g_in), (h_hbm, h_in), (r_hbm, r_in), (u_hbm, u_in), (q_hbm, q_in),
                 (ve_hbm, ve_ref), (oe_hbm, oe_ref), (se_hbm, se_ref), (t_hbm, t_ref),
             )
         )
@@ -384,75 +379,59 @@
     for load in loads:
         load.start()
     barrier = pltpu.get_barrier_semaphore()
-    near = [here.along_b(0, 1), here.along_b(0, 7), here.along_b(1, 0)]
+    near = [here.along_b(0, k) for k in range(1, 8)] + [here.along_b(1, 0)]
     near += [here.along_a(0, d, 0) for d in range(1, 4)]
     near += [here.along_a(1, 0, 0), here.along_a(0, 0, 1)]
     for target in near:
         pl.semaphore_signal(barrier, inc=1, device_id=target, device_id_type=MESH)
-    for load in loads[:5]:
+    for load in loads[:4]:
         load.wait()
     own_col = cols.at[pl.ds(pl.multiple_of(here.a * CHUNK, 16), CHUNK), :]
-    split_l(
-        g_in, h_in, q_in, r_in, u_in, rows.at[0:CHUNK, :], own_col, q_ref, amp
-    )
+    split_l(g_in, h_in, r_in, u_in, rows.at[0:CHUNK, :], own_col, amp)
     pl.semaphore_wait(barrier, len(near))
     net = Gather(here, rows, cols, gather_sems, row_sems, col_sems)
-    net.swap_row()
-    net.up(0, 0)
-    net.down(0, 0)
+    net.across_x(0)
+    for k in ORDER:
+        net.along_z(k)
     net.swap_col()
     net.round_col(0)
     net.twin_col(0, 0)
-    clear_off(bdh, bdu)
-    for load in loads[5:]:
+    for load in loads[4:]:
         load.wait()
-    compute_a(here, t_ref, q_ref, a_ref, 0, 2)
-    net.got_row(0, 1)
-    net.up(0, 1)
-    net.got_row(0, 7)
-    net.down(0, 7)
-    net.got_row(1, 0)
-    net.up(1, 0)
-    net.down(1, 0)
+    split_q(q_in, q_ref)
     net.got_col(1, 0)
     net.round_col(1)
     net.twin_col(1, 0)
-    compute_a(here, t_ref, q_ref, a_ref, 2, 3)
-    net.got_row(0, 2)
-    net.up(0, 2)
-    net.got_row(0, 6)
-    net.down(0, 6)
+    compute_a(here, t_ref, q_ref, a_ref, 0, 4)
+    for k in ORDER[0:2]:
+        net.got_row(0, k)
+        net.across_x(k)
     for d in range(1, 4):
         net.got_col(0, d)
         net.twin_col(0, d)
-    compute_a(here, t_ref, q_ref, a_ref, 5, 3)
-    net.got_row(1, 1)
-    net.up(1, 1)
-    net.got_row(1, 7)
-    net.down(1, 7)
+    compute_a(here, t_ref, q_ref, a_ref, 4, 4)
+    for k in ORDER[2:4]:
+        net.got_row(0, k)
+        net.across_x(k)
     for d in range(1, 4):
         net.got_col(1, d)
         net.twin_col(1, d)
-    compute_a(here, t_ref, q_ref, a_ref, 8, 3)
-    net.got_row(0, 3)
-    net.up(0, 3)
-    net.got_row(0, 5)
-    compute_a(here, t_ref, q_ref, a_ref, 11, 3)
-    net.got_row(1, 2)
-    net.up(1, 2)
-    net.got_row(1, 6)
-    net.down(1, 6)
-    compute_a(here, t_ref, q_ref, a_ref, 14, 2)
-    net.got_row(1, 3)
-    net.got_row(1, 5)
-    net.down(1, 5)
+    compute_a(here, t_ref, q_ref, a_ref, 8, 4)
+    for k in ORDER[4:6]:
+        net.got_row(0, k)
+        net.across_x(k)
+    compute_a(here, t_ref, q_ref, a_ref, 12, 4)
+    for k in ORDER[6:]:
+        net.got_row(0, k)
+        net.across_x(k)
+    clear_off(bdh, bdu)
     for kind in (2, 3):
         for d in range(4):
             net.got_col(kind, d)
     spread(cols, functools.partial(put_cols, bdh, bdu))
     base = pair_energy(here, ve_ref)
-    net.got_row(0, 4)
-    net.got_row(1, 4)
+    for k in range(8):
+        net.got_row(1, k)
     spread(rows, functools.partial(put_rows, g2, r2))
     for copy in net.sent:
         copy.wait_send()
@@ -461,24 +440,24 @@
     sums = [[], []]
     for s in range(NC):
         weigh(oe_ref, se_ref, base, s, a_ref, p_ref, c_ref, yr, yc)
-        row_residual(s, bdh, yr, res, row_part.at[s])
+        row_residual(s, bdh, yr, res, wide, row_part.at[s])
         sums[0] += scatter(here, s, True, row_part, row_into, out_row_sems, sum_row_sems)
     for s in range(NC):
-        col_residual(s, turned, yc, res, col_part.at[s])
+        col_residual(s, turned, yc, res, wide, col_part.at[s])
         sums[1] += scatter(here, s, False, col_part, col_into, out_col_sems, sum_col_sems)
     for which, (part, into, out, own) in enumerate(
         (
-            (col_part, col_into, col_out, pl.multiple_of(here.a * PART, 8)),
+            (col_part, col_into, col_out, here.a),
             (row_part, row_into, row_out, 0),
         )
     ):
         for s in range(NC):
-            total = part[s, pl.ds(own, PART), :]
+            total = part[s, own]
             for n in range(1, GROUP):
                 sums[1 - which][s * (GROUP - 1) + n - 1].wait_recv()
-                total = total + into[s, n * PART : (n + 1) * PART, :]
-            last[pl.ds(s, PART, stride=NC), :] = total * factor
-        out[...] = last[0 : NC * USED, :]
+                total = total + into[s, n]
+            last[pl.ds(s, USED, stride=NC), :] = total
+        out[...] = last[...]
     for copy in sums[0] + sums[1]:
         copy.wait_send()
 
@@ -502,20 +481,20 @@
     operands = (
         t, row_integral, column_integral, step_integral, r, u, ve, occupied_energy, step_energy
     )
-    out = jax.ShapeDtypeStruct((NC * USED, NO), F32)
+    out = pltpu.VMEM((NC * USED, NO), F32)
     vm = pl.BlockSpec(memory_space=pltpu.VMEM)
     spaces = [pltpu.VMEM] * 7 + [pltpu.SMEM] * 2
-    order = (0, 1, 2, 3, 4, 5, 6, 7, 8)
+    order = range(9)
     dma = pltpu.SemaphoreType.DMA
     results = pl.pallas_call(
-        functools.partial(whole_body, factor),
+        whole_body,
         out_shape=(out, out),
         in_specs=[pl.BlockSpec(memory_space=pl.ANY)] * 9,
         out_specs=(vm, vm),
         scratch_shapes=[spaces[n](operands[n].shape, operands[n].dtype) for n in order]
         + [
             pltpu.VMEM((64, NO), BF16),
-            pltpu.VMEM((OWN * SI, NO), F32),
+            pltpu.VMEM((2, OWN * SI, NO), F32),
             pltpu.VMEM((GROUP * CHUNK, NO), BF16),
             pltpu.VMEM((GROUP * CHUNK, NO), BF16),
             pltpu.VMEM((32 * OT * AROWS, NO), F32),
@@ -529,11 +508,12 @@
             pltpu.VMEM((SI * 800, NO), BF16),
             pltpu.VMEM((2 * NO, 800), BF16),
             pltpu.VMEM((OT * 64, NO), F32),
-            pltpu.VMEM((NC, GROUP * PART, NO), F32),
-            pltpu.VMEM((NC, GROUP * PART, NO), F32),
-            pltpu.VMEM((NC, GROUP * PART, NO), F32),
-            pltpu.VMEM((NC, GROUP * PART, NO), F32),
-            pltpu.VMEM((NC * PART, NO), F32),
+            pltpu.VMEM((GROUP * PART, NO), F32),
+            pltpu.VMEM((NC, GROUP, USED, NO), F32),
+            pltpu.VMEM((NC, GROUP, USED, NO), F32),
+            pltpu.VMEM((NC, GROUP, USED, NO), F32),
+            pltpu.VMEM((NC, GROUP, USED, NO), F32),
+            pltpu.VMEM((NC * USED, NO), F32),
             dma((9,)),
             dma((30,)),
             dma((2, 8)),
@@ -548,7 +528,7 @@
         ),
     )(*operands)
     return tuple(
-        x.reshape(OWN, OT, NC, NO).transpose(0, 2, 1, 3) for x in results
+        (x * factor).reshape(OWN, OT, NC, NO).transpose(0, 2, 1, 3) for x in results
     )
 
 

time: 46.7 us -> 39.9 us (0.85)
  Pallas kernels: 43.2 us -> 38.5 us
  local copies, waits for them, and re-layouts: 2.67 us -> 0 us
  other arithmetic: 0 us -> 0.62 us
    pallas_call x1, Pallas kernels: 43.2 us -> 38.5 us  [on_device(): pl.pallas_call(whole_body, out_shape=(out, out), in_specs=[pl.BlockSpec(m...]
    unnamed x2 -> x0, local copies, waits for them, and re-layouts: 2.67 us -> none
    mul x0 -> x1, other arithmetic: none -> 0.62 us  [on_device(): x * factor]
where the time goes in v3:
time: 39.9 us; the launch traced here: 39.8 us
  Pallas kernels  38.5 us (96%)
  between operations  0.64 us (2%)
  other arithmetic  0.62 us (2%)
    pallas_call x1, Pallas kernels, on_device(): pl.pallas_call(whole_body, out_shape=(out, out), in_specs=[pl.BlockSpec(m...  38.5 us

profile of v3, /device:TPU:1, one launch (start us, length us, event | category | flops | bytes accessed | tf_op | source)
XLA Modules:
  0.0 39.8 jit_solution(15656636800608569713)
XLA Ops:
  0.6 38.5 %shard_map.104 = (f32[40,128]{1,0:T(8,128)S(1)}, f32[40,128]{1,0:T(8,128)S(1)}) custom-call(bf16[64,5,64,128]{3,2,1,0:T(8,128)(2,1)} %bitcast.14, bf16[4,3200]{1,0:T(4,128)(2,1)} %g_hbm.1, bf16[4,3200]{1,0:T(4,128)(2,1)} %h_hbm.1, bf16[2,3200]{1,0:T(2,128)(2,1)} %q_hbm.1, bf16[40,128]{1,0:T(8,128)(2,1)} %bitcast.17, bf16[40,128]{1,0:T(8,128)(2,1)} %bitcast.18, ...), custom_call_target="tpu_custom_call" | custom-call | tf_op jit(solution)/shard_map/pallas_call | solution.py:489
  39.1 0.6 %broadcast_multiply_fusion = (f32[40,128]{1,0:T(8,128)}, f32[40,128]{1,0:T(8,128)}) fusion(f32[40,128]{1,0:T(8,128)S(1)} %get-tuple-element.5, f32[40,128]{1,0:T(8,128)S(1)} %get-tuple-element.4), kind=kLoop, calls=%fused_computation | loop fusion | flops 10240 | bytes 81920 | tf_op jit(solution)/shard_map/mul | solution.py:531

commit v4 on v3

--- a/solution.py
+++ b/solution.py
@@ -21,7 +21,8 @@
 CHUNK = 144
 PART = 24
 USED = OWN * OT
-ORDER = (1, 7, 2, 6, 3, 5, 4)
+ORDER = (0, 1, 7, 2, 6, 3, 5, 4)
+HALF = 4
 AROWS = 56
 NT = (((1,), (1,)), ((), ()))
 
@@ -109,30 +110,36 @@
 
 def compute_a(here, t_ref, q_ref, a_out, first, count):
     q = q_ref[0:AROWS, :]
-
-    def pair(n, _):
-        at_k = n // 2
-        v = 2 * lax.rem(n, 2)
-        zk = lax.rem(here.z - at_k + 8, 8)
-        near = (here.xh * 8 + zk) * OWN + v
-        far = ((1 - here.xh) * 8 + zk) * OWN + v
-        for i in range(OT):
-            block = jnp.concatenate(
-                [t_ref[near, i], t_ref[far, i], t_ref[near + 1, i], t_ref[far + 1, i]], 0
-            )
-            part = dot_nt(q, block)
-            for half in range(2):
-                at = pl.multiple_of((2 * n + half) * (OT * AROWS) + i * AROWS, 8)
-                a_out[pl.ds(at, AROWS), :] = part[:, half * NO : (half + 1) * NO]
-        return 0
-
-    lax.fori_loop(first, first + count, pair, 0)
+    for at_k in range(first, first + count):
+        zk = lax.rem(here.z - ORDER[at_k] + 8, 8)
+        near_k = (here.xh * 8 + zk) * OWN
+        far_k = ((1 - here.xh) * 8 + zk) * OWN
+
+        def pair(n, _, at_k=at_k, near_k=near_k, far_k=far_k):
+            near, far = near_k + 2 * n, far_k + 2 * n
+            for i in range(OT):
+                block = jnp.concatenate(
+                    [t_ref[near, i], t_ref[far, i], t_ref[near + 1, i], t_ref[far + 1, i]],
+                    0,
+                )
+                part = dot_nt(q, block)
+                for half in range(2):
+                    at = pl.multiple_of(
+                        (4 * at_k + 2 * n + half) * (OT * AROWS) + i * AROWS, 8
+                    )
+                    a_out[pl.ds(at, AROWS), :] = part[:, half * NO : (half + 1) * NO]
+            return 0
+
+        lax.fori_loop(0, 2, pair, 0)
 
 
 def pair_energy(here, ve_ref):
     lane = lax.broadcasted_iota(jnp.int32, (32, NO), 1)
     row = lax.broadcasted_iota(jnp.int32, (32, NO), 0)
-    zk = (here.z - (row >> 2)) & 7
+    offset = jnp.zeros((32, NO), jnp.int32)
+    for at_k, k in enumerate(ORDER):
+        offset = jnp.where((row >> 2) == at_k, k, offset)
+    zk = (here.z - offset) & 7
     lead = jnp.broadcast_to(ve_ref[pl.ds(here.a // 2, 1), :], (32, NO))
     first = lax.rem(here.a, 2) * 64
     halves = []
@@ -160,10 +167,20 @@
             wide(at, tile.astype(BF16))
 
 
-def put_rows(g2, r2, at, tile):
-    dst, c = (g2, at) if at < JK else (r2, at - JK)
-    dst[c * 32 : c * 32 + 32, 0:NO] = tile[0:32]
-    dst[c * 32 : c * 32 + 32, NO : 2 * NO] = tile[32:64]
+def spread_rows(group, rows, g2, r2):
+    for k in range(9):
+        for q in range(2):
+            blocks = []
+            for offset in ORDER[group * HALF : (group + 1) * HALF]:
+                at = (q * 8 + offset) * CHUNK + 16 * k
+                blocks.append(rows[at : at + 16, :].astype(F32))
+            for c in range(4):
+                at = 4 * k + c
+                if at >= JK + SI:
+                    continue
+                tile = jnp.concatenate([b[4 * c : 4 * c + 4] for b in blocks], 0)
+                dst, to = (g2, at) if at < JK else (r2, at - JK)
+                dst[to * 16 : to * 16 + 16, q * NO : (q + 1) * NO] = tile.astype(BF16)
 
 
 def put_cols(bdh, bdu, at, tile):
@@ -182,25 +199,21 @@
 
 def compute_pc(g2, r2, bdh, bdu, p_out, c_out):
     r = r2[...]
-
     for n in range(JK // 2 + 1):
         width = 2 if n < JK // 2 else 1
         part = dot_nt(r, bdh[2 * n * NO : (2 * n + width) * NO, :])
         for half in range(width):
-            p_out[(2 * n + half) * 320 : (2 * n + half + 1) * 320, :] = part[
+            p_out[(2 * n + half) * 160 : (2 * n + half + 1) * 160, :] = part[
                 :, half * NO : (half + 1) * NO
             ]
     for n in range(OT):
-        for m in range(5):
-            part = dot_nt(
-                g2[m * 160 : (m + 1) * 160, :], bdu[2 * n * NO : (2 * n + 2) * NO, :]
-            )
-            for half in range(2):
-                at = (2 * n + half) * 800 + m * 160
-                c_out[at : at + 160, :] = part[:, half * NO : (half + 1) * NO]
-
-
-def weigh(oe_ref, se_ref, base, s, a_in, p_in, c_in, yr, yc):
+        part = dot_nt(g2[...], bdu[2 * n * NO : (2 * n + 2) * NO, :])
+        for half in range(2):
+            at = (2 * n + half) * 400
+            c_out[at : at + 400, :] = part[:, half * NO : (half + 1) * NO]
+
+
+def weigh(oe_ref, se_ref, base, group, s, a_in, p_in, c_in, yr, yc):
     start = base + se_ref[s]
 
     def one(i, _):
@@ -211,24 +224,25 @@
                 ij = i * OT + j
                 energy = (oe_ref[i] + oe_ref[j]) + oe_ref[k]
                 tiles = []
-                for v in range(4):
-                    first = v * 8 * OT * AROWS + s * JK
+                for v in range(2):
+                    row = group * 16 + v * 8
+                    first = row * OT * AROWS + s * JK
                     w = a_in[pl.ds(first + i * AROWS + jk, 8, stride=OT * AROWS), :]
                     w = w + a_in[pl.ds(first + j * AROWS + ki, 8, stride=OT * AROWS), :]
-                    at = pl.multiple_of(jk * 320 + (s * OT + i) * 32 + v * 8, 8)
+                    at = pl.multiple_of(jk * 160 + (s * OT + i) * 16 + v * 8, 8)
                     w = w + p_in[pl.ds(at, 8), :]
-                    at = pl.multiple_of(ij * 320 + (s * OT + k) * 32 + v * 8, 8)
+                    at = pl.multiple_of(ij * 160 + (s * OT + k) * 16 + v * 8, 8)
                     w = w + p_in[pl.ds(at, 8), :]
-                    at = pl.multiple_of((s * OT + j) * 800 + ki * 32 + v * 8, 8)
+                    at = pl.multiple_of((s * OT + j) * 400 + ki * 16 + v * 8, 8)
                     w = w + c_in[pl.ds(at, 8), :]
-                    at = pl.multiple_of((s * OT + k) * 800 + ij * 32 + v * 8, 8)
+                    at = pl.multiple_of((s * OT + k) * 400 + ij * 16 + v * 8, 8)
                     w = w + c_in[pl.ds(at, 8), :]
-                    tiles.append(w / (start[v * 8 : v * 8 + 8] - energy))
+                    tiles.append(w / (start[row : row + 8] - energy))
                 y = jnp.concatenate(tiles, 0).astype(BF16)
-                at = pl.multiple_of((s * OT + i) * 32, 32)
-                yr[pl.ds(at, 32), jk * NO : (jk + 1) * NO] = y
-                at = pl.multiple_of((s * OT + j) * 800 + ki * 32, 32)
-                yc[pl.ds(at, 32), :] = y
+                at = pl.multiple_of((s * OT + i) * 16, 16)
+                yr[pl.ds(at, 16), jk * NO : (jk + 1) * NO] = y
+                at = pl.multiple_of((s * OT + j) * 400 + ki * 16, 16)
+                yc[pl.ds(at, 16), :] = y
         return 0
 
     lax.fori_loop(0, OT, one, 0)
@@ -244,25 +258,39 @@
         out[n] = wide[n * PART : n * PART + USED, :]
 
 
-def row_residual(s, bdh, yr, res, wide, row_out):
-    out = jnp.dot(yr[s * 160 : (s + 1) * 160, :], bdh[...], preferred_element_type=F32)
-    for i in range(OT):
-        for half in range(2):
-            res[i * 64 + half * 32 : i * 64 + half * 32 + 32, :] = out[
-                i * 32 : i * 32 + 32, half * NO : (half + 1) * NO
+def row_residual(bdh, yr, res, row_out):
+    out = jnp.dot(yr[...], bdh[...], preferred_element_type=F32)
+    for c in range(SI):
+        for q in range(2):
+            res[c * 32 + q * 16 : c * 32 + q * 16 + 16, :] = out[
+                c * 16 : c * 16 + 16, q * NO : (q + 1) * NO
             ]
-    deal(res, wide, row_out)
-
-
-def col_residual(s, turned, yc, res, wide, col_out):
+    for c in range(SI):
+        for v in range(OWN):
+            at = v * SI + c % OT * NC + c // OT
+            row_out[pl.ds(at, 2 * HALF, stride=OWN * SI), :] = res[
+                pl.ds(c * 32 + v, 2 * HALF, stride=OWN), :
+            ]
+
+
+def col_products(s, turned, yc):
     lane = lax.broadcasted_iota(jnp.int32, (NO, NO), 1)
     moved = jnp.concatenate(
-        [yc[(s * OT + j) * 800 : (s * OT + j + 1) * 800, :] for j in range(OT)], 1
+        [yc[(s * OT + j) * 400 : (s * OT + j + 1) * 400, :] for j in range(OT)], 1
     )
-    out = jnp.dot(turned[...], moved, preferred_element_type=F32)
-    for j in range(OT):
-        piece = out[:, j * NO : (j + 1) * NO]
-        both = jnp.where(lane < 64, piece[0:NO], piece[NO:]).T
+    out = jnp.dot(turned, moved, preferred_element_type=F32)
+    pieces = [out[:, j * NO : (j + 1) * NO] for j in range(OT)]
+    return [jnp.where(lane < 64, piece[0:NO], piece[NO:]) for piece in pieces]
+
+
+def col_first(s, turned, yc, held):
+    for j, piece in enumerate(col_products(s, turned, yc)):
+        held[s * OT + j] = piece
+
+
+def col_residual(s, turned, yc, held, res, wide, col_out):
+    for j, piece in enumerate(col_products(s, turned, yc)):
+        both = (piece + held[s * OT + j]).T
         res[j * 64 : j * 64 + 64, :] = both[0:64] + both[64:128]
     deal(res, wide, col_out)
 
@@ -335,25 +363,46 @@
         ).wait_recv()
 
 
-def scatter(here, s, along_rows, part, into, send_sems, recv_sems):
+def send_part(src, dst, send_sem, recv_sem, target):
+    copy = pltpu.make_async_remote_copy(
+        src_ref=src,
+        dst_ref=dst,
+        send_sem=send_sem,
+        recv_sem=recv_sem,
+        device_id=target,
+        device_id_type=MESH,
+    )
+    copy.start()
+    return copy
+
+
+def scatter_rows(here, group, part, into, send_sems, recv_sems):
+    copies = []
+    for q in (1, 0):
+        for p in reversed(range(HALF)):
+            k = ORDER[group * HALF + p]
+            if q == 0 and k == 0:
+                continue
+            at = (q * HALF + p) * OWN * SI
+            copies.append(
+                send_part(
+                    part.at[group, at : at + OWN * SI, :], into.at[q * 8 + k],
+                    send_sems.at[q * 8 + k], recv_sems.at[q * 8 + k], here.along_b(q, k),
+                )
+            )
+    return copies
+
+
+def scatter_cols(here, s, part, into, send_sems, recv_sems):
     copies = []
     for n in range(1, GROUP):
-        if along_rows:
-            target = here.along_b(n // 8, n % 8)
-            at = n
-        else:
-            target = here.along_a(n // 8, n // 2 % 4, n % 2)
-            at = target[0]
-        copy = pltpu.make_async_remote_copy(
-            src_ref=part.at[s, at],
-            dst_ref=into.at[s, n],
-            send_sem=send_sems.at[s, n],
-            recv_sem=recv_sems.at[s, n],
-            device_id=target,
-            device_id_type=MESH,
+        target = here.along_a(n // 8, n // 2 % 4, n % 2)
+        copies.append(
+            send_part(
+                part.at[s, target[0]], into.at[s, n], send_sems.at[s, n],
+                recv_sems.at[s, n], target,
+            )
         )
-        copy.start()
-        copies.append(copy)
     return copies
 
 
@@ -361,7 +410,7 @@
     t_hbm, g_hbm, h_hbm, q_hbm, r_hbm, u_hbm, ve_hbm, oe_hbm, se_hbm,
     row_out, col_out,
     t_ref, g_in, h_in, q_in, r_in, u_in, ve_ref, oe_ref, se_ref,
-    q_ref, amp, rows, cols, a_ref, g2, r2, bdh, bdu, p_ref, c_ref, yr, yc, turned, res, wide,
+    q_ref, amp, rows, cols, a_ref, g2, r2, bdh, bdu, p_ref, c_ref, yr, yc, res, wide, held,
     row_part, col_part, row_into, col_into, last,
     in_sems, gather_sems, row_sems, col_sems, out_row_sems, out_col_sems, sum_row_sems,
     sum_col_sems,
@@ -392,7 +441,8 @@
     net = Gather(here, rows, cols, gather_sems, row_sems, col_sems)
     net.across_x(0)
     for k in ORDER:
-        net.along_z(k)
+        if k:
+            net.along_z(k)
     net.swap_col()
     net.round_col(0)
     net.twin_col(0, 0)
@@ -402,26 +452,27 @@
     net.got_col(1, 0)
     net.round_col(1)
     net.twin_col(1, 0)
-    compute_a(here, t_ref, q_ref, a_ref, 0, 4)
-    for k in ORDER[0:2]:
+    compute_a(here, t_ref, q_ref, a_ref, 0, 2)
+    others = [k for k in ORDER if k]
+    for k in others[0:2]:
         net.got_row(0, k)
         net.across_x(k)
     for d in range(1, 4):
         net.got_col(0, d)
         net.twin_col(0, d)
-    compute_a(here, t_ref, q_ref, a_ref, 4, 4)
-    for k in ORDER[2:4]:
+    compute_a(here, t_ref, q_ref, a_ref, 2, 2)
+    for k in others[2:4]:
         net.got_row(0, k)
         net.across_x(k)
     for d in range(1, 4):
         net.got_col(1, d)
         net.twin_col(1, d)
-    compute_a(here, t_ref, q_ref, a_ref, 8, 4)
-    for k in ORDER[4:6]:
+    compute_a(here, t_ref, q_ref, a_ref, 4, 2)
+    for k in others[4:6]:
         net.got_row(0, k)
         net.across_x(k)
-    compute_a(here, t_ref, q_ref, a_ref, 12, 4)
-    for k in ORDER[6:]:
+    compute_a(here, t_ref, q_ref, a_ref, 6, 2)
+    for k in others[6:]:
         net.got_row(0, k)
         net.across_x(k)
     clear_off(bdh, bdu)
@@ -430,35 +481,44 @@
             net.got_col(kind, d)
     spread(cols, functools.partial(put_cols, bdh, bdu))
     base = pair_energy(here, ve_ref)
-    for k in range(8):
-        net.got_row(1, k)
-    spread(rows, functools.partial(put_rows, g2, r2))
+    row_sums, col_sums = [], []
+    for group in range(2):
+        for k in ORDER[group * HALF : (group + 1) * HALF]:
+            net.got_row(1, k)
+        spread_rows(group, rows, g2, r2)
+        compute_pc(g2, r2, bdh, bdu, p_ref, c_ref)
+        for s in range(NC):
+            weigh(oe_ref, se_ref, base, group, s, a_ref, p_ref, c_ref, yr, yc)
+        row_residual(bdh, yr, res, row_part.at[group])
+        row_sums += scatter_rows(
+            here, group, row_part, row_into, out_row_sems, sum_row_sems
+        )
+        turned = g2[...].T
+        for s in range(NC):
+            if group == 0:
+                col_first(s, turned, yc, held)
+                continue
+            col_residual(s, turned, yc, held, res, wide, col_part.at[s])
+            col_sums += scatter_cols(
+                here, s, col_part, col_into, out_col_sems, sum_col_sems
+            )
     for copy in net.sent:
         copy.wait_send()
-    compute_pc(g2, r2, bdh, bdu, p_ref, c_ref)
-    turned[...] = g2[...].T
-    sums = [[], []]
     for s in range(NC):
-        weigh(oe_ref, se_ref, base, s, a_ref, p_ref, c_ref, yr, yc)
-        row_residual(s, bdh, yr, res, wide, row_part.at[s])
-        sums[0] += scatter(here, s, True, row_part, row_into, out_row_sems, sum_row_sems)
-    for s in range(NC):
-        col_residual(s, turned, yc, res, wide, col_part.at[s])
-        sums[1] += scatter(here, s, False, col_part, col_into, out_col_sems, sum_col_sems)
-    for which, (part, into, out, own) in enumerate(
-        (
-            (col_part, col_into, col_out, here.a),
-            (row_part, row_into, row_out, 0),
-        )
-    ):
-        for s in range(NC):
-            total = part[s, own]
-            for n in range(1, GROUP):
-                sums[1 - which][s * (GROUP - 1) + n - 1].wait_recv()
-                total = total + into[s, n]
-            last[pl.ds(s, USED, stride=NC), :] = total
-        out[...] = last[...]
-    for copy in sums[0] + sums[1]:
+        total = col_part[s, here.a]
+        for n in range(1, GROUP):
+            col_sums[s * (GROUP - 1) + n - 1].wait_recv()
+            total = total + col_into[s, n]
+        last[pl.ds(s, USED, stride=NC), :] = total
+    col_out[...] = last[...]
+    at = ORDER.index(0)
+    total = row_part[at // HALF, at % HALF * OWN * SI : (at % HALF + 1) * OWN * SI, :]
+    for copy in row_sums:
+        copy.wait_recv()
+    for n in range(1, GROUP):
+        total = total + row_into[n]
+    row_out[...] = total
+    for copy in row_sums + col_sums:
         copy.wait_send()
 
 
@@ -498,29 +558,29 @@
             pltpu.VMEM((GROUP * CHUNK, NO), BF16),
             pltpu.VMEM((GROUP * CHUNK, NO), BF16),
             pltpu.VMEM((32 * OT * AROWS, NO), F32),
-            pltpu.VMEM((JK * 32, 2 * NO), BF16),
-            pltpu.VMEM((SI * 32, 2 * NO), BF16),
+            pltpu.VMEM((JK * 16, 2 * NO), BF16),
+            pltpu.VMEM((SI * 16, 2 * NO), BF16),
             pltpu.VMEM((JK * NO, 2 * NO), BF16),
             pltpu.VMEM((SI * NO, 2 * NO), BF16),
-            pltpu.VMEM((JK * 320, NO), F32),
-            pltpu.VMEM((SI * 800, NO), F32),
-            pltpu.VMEM((320, JK * NO), BF16),
-            pltpu.VMEM((SI * 800, NO), BF16),
-            pltpu.VMEM((2 * NO, 800), BF16),
+            pltpu.VMEM((JK * 160, NO), F32),
+            pltpu.VMEM((SI * 400, NO), F32),
+            pltpu.VMEM((160, JK * NO), BF16),
+            pltpu.VMEM((SI * 400, NO), BF16),
             pltpu.VMEM((OT * 64, NO), F32),
             pltpu.VMEM((GROUP * PART, NO), F32),
+            pltpu.VMEM((SI, NO, NO), F32),
+            pltpu.VMEM((2, 2 * HALF * OWN * SI, NO), F32),
             pltpu.VMEM((NC, GROUP, USED, NO), F32),
-            pltpu.VMEM((NC, GROUP, USED, NO), F32),
-            pltpu.VMEM((NC, GROUP, USED, NO), F32),
+            pltpu.VMEM((GROUP, OWN * SI, NO), F32),
             pltpu.VMEM((NC, GROUP, USED, NO), F32),
             pltpu.VMEM((NC * USED, NO), F32),
             dma((9,)),
             dma((30,)),
             dma((2, 8)),
             dma((4, 4)),
+            dma((GROUP,)),
             dma((NC, GROUP)),
-            dma((NC, GROUP)),
-            dma((NC, GROUP)),
+            dma((GROUP,)),
             dma((NC, GROUP)),
         ],
         compiler_params=pltpu.CompilerParams(

time: 39.9 us -> 38 us (0.952)
  Pallas kernels: 38.5 us -> 36.7 us
    pallas_call x1, Pallas kernels: 38.5 us -> 36.7 us  [on_device(): pl.pallas_call(whole_body, out_shape=(out, out), in_specs=[pl.BlockSpec(m...]
where the time goes in v4:
time: 38 us; the launch traced here: 37.9 us
  Pallas kernels  36.7 us (97%)
  between operations  0.64 us (2%)
  other arithmetic  0.62 us (2%)
    pallas_call x1, Pallas kernels, on_device(): pl.pallas_call(whole_body, out_shape=(out, out), in_specs=[pl.BlockSpec(m...  36.7 us

profile of v4, /device:TPU:1, one launch (start us, length us, event | category | flops | bytes accessed | tf_op | source)
XLA Modules:
  0.0 37.9 jit_solution(11738734455091611334)
XLA Ops:
  0.6 36.7 %shard_map.104 = (f32[40,128]{1,0:T(8,128)S(1)}, f32[40,128]{1,0:T(8,128)S(1)}) custom-call(bf16[64,5,64,128]{3,2,1,0:T(8,128)(2,1)} %bitcast.14, bf16[4,3200]{1,0:T(4,128)(2,1)} %g_hbm.1, bf16[4,3200]{1,0:T(4,128)(2,1)} %h_hbm.1, bf16[2,3200]{1,0:T(2,128)(2,1)} %q_hbm.1, bf16[40,128]{1,0:T(8,128)(2,1)} %bitcast.17, bf16[40,128]{1,0:T(8,128)(2,1)} %bitcast.18, ...), custom_call_target="tpu_custom_call" | custom-call | tf_op jit(solution)/shard_map/pallas_call | solution.py:549
  37.3 0.6 %broadcast_multiply_fusion = (f32[40,128]{1,0:T(8,128)}, f32[40,128]{1,0:T(8,128)}) fusion(f32[40,128]{1,0:T(8,128)S(1)} %get-tuple-element.5, f32[40,128]{1,0:T(8,128)S(1)} %get-tuple-element.4), kind=kLoop, calls=%fused_computation | loop fusion | flops 10240 | bytes 81920 | tf_op jit(solution)/shard_map/mul | solution.py:591

commit v5 on v4

--- a/solution.py
+++ b/solution.py
@@ -19,7 +19,6 @@
 SI = OT * NC
 NO = 128
 CHUNK = 144
-PART = 24
 USED = OWN * OT
 ORDER = (0, 1, 7, 2, 6, 3, 5, 4)
 HALF = 4
@@ -213,49 +212,42 @@
             c_out[at : at + 400, :] = part[:, half * NO : (half + 1) * NO]
 
 
+def cycles():
+    found, seen = [], set()
+    for n in range(OT**3):
+        i, j, k = n // JK, n // OT % OT, n % OT
+        if (i, j, k) not in seen:
+            turns = [(i, j, k), (j, k, i), (k, i, j)]
+            found.append(turns if i != j or j != k else turns[:1])
+            seen.update(turns)
+    return found
+
+
 def weigh(oe_ref, se_ref, base, group, s, a_in, p_in, c_in, yr, yc):
-    start = base + se_ref[s]
-
-    def one(i, _):
-        for j in range(OT):
-            for k in range(OT):
-                jk = j * OT + k
-                ki = k * OT + i
-                ij = i * OT + j
-                energy = (oe_ref[i] + oe_ref[j]) + oe_ref[k]
-                tiles = []
-                for v in range(2):
-                    row = group * 16 + v * 8
-                    first = row * OT * AROWS + s * JK
-                    w = a_in[pl.ds(first + i * AROWS + jk, 8, stride=OT * AROWS), :]
-                    w = w + a_in[pl.ds(first + j * AROWS + ki, 8, stride=OT * AROWS), :]
-                    at = pl.multiple_of(jk * 160 + (s * OT + i) * 16 + v * 8, 8)
-                    w = w + p_in[pl.ds(at, 8), :]
-                    at = pl.multiple_of(ij * 160 + (s * OT + k) * 16 + v * 8, 8)
-                    w = w + p_in[pl.ds(at, 8), :]
-                    at = pl.multiple_of((s * OT + j) * 400 + ki * 16 + v * 8, 8)
-                    w = w + c_in[pl.ds(at, 8), :]
-                    at = pl.multiple_of((s * OT + k) * 400 + ij * 16 + v * 8, 8)
-                    w = w + c_in[pl.ds(at, 8), :]
-                    tiles.append(w / (start[row : row + 8] - energy))
-                y = jnp.concatenate(tiles, 0).astype(BF16)
-                at = pl.multiple_of((s * OT + i) * 16, 16)
-                yr[pl.ds(at, 16), jk * NO : (jk + 1) * NO] = y
-                at = pl.multiple_of((s * OT + j) * 400 + ki * 16, 16)
-                yc[pl.ds(at, 16), :] = y
-        return 0
-
-    lax.fori_loop(0, OT, one, 0)
-
-
-def deal(res, wide, out):
-    for i in range(OT):
-        for v in range(OWN):
-            wide[pl.ds(v * OT + i, GROUP, stride=PART), :] = res[
-                pl.ds(i * 64 + v, GROUP, stride=OWN), :
-            ]
-    for n in range(GROUP):
-        out[n] = wide[n * PART : n * PART + USED, :]
+    start = base[group * 16 : group * 16 + 16] + se_ref[s]
+    first = group * 16 * OT * AROWS + s * JK
+    for turns in cycles():
+        i, j, k = turns[0]
+        inverse = 1.0 / (start - ((oe_ref[i] + oe_ref[j]) + oe_ref[k]))
+        a, p, c = [], [], []
+        for x, y, z in turns:
+            yz = y * OT + z
+            at = first + x * AROWS + yz
+            a.append(a_in[pl.ds(at, 16, stride=OT * AROWS), :])
+            at = yz * 160 + (s * OT + x) * 16
+            p.append(p_in[at : at + 16, :])
+            at = (s * OT + x) * 400 + yz * 16
+            c.append(c_in[at : at + 16, :])
+        count = len(turns)
+        for n, (x, y, z) in enumerate(turns):
+            one, two = (n + 1) % count, (n + 2) % count
+            w = (a[n] + a[one]) + (p[n] + p[two]) + (c[one] + c[two])
+            out = (w * inverse).astype(BF16)
+            yz = y * OT + z
+            at = (s * OT + x) * 16
+            yr[at : at + 16, yz * NO : (yz + 1) * NO] = out
+            at = (s * OT + y) * 400 + (z * OT + x) * 16
+            yc[at : at + 16, :] = out
 
 
 def row_residual(bdh, yr, res, row_out):
@@ -288,11 +280,16 @@
         held[s * OT + j] = piece
 
 
-def col_residual(s, turned, yc, held, res, wide, col_out):
+def col_residual(s, turned, yc, held, res, col_out):
     for j, piece in enumerate(col_products(s, turned, yc)):
         both = (piece + held[s * OT + j]).T
         res[j * 64 : j * 64 + 64, :] = both[0:64] + both[64:128]
-    deal(res, wide, col_out)
+    for j in range(OT):
+        for core in range(2):
+            for v in range(OWN):
+                col_out[core, pl.ds(v * SI + j * NC + s, 8, stride=OWN * SI), :] = res[
+                    pl.ds(j * 64 + core * OWN + v, 8, stride=2 * OWN), :
+                ]
 
 
 class Gather:
@@ -393,14 +390,15 @@
     return copies
 
 
-def scatter_cols(here, s, part, into, send_sems, recv_sems):
+def scatter_cols(here, part, into, send_sems, recv_sems):
     copies = []
-    for n in range(1, GROUP):
-        target = here.along_a(n // 8, n // 2 % 4, n % 2)
+    for n in (6, 5, 7, 2, 1, 3, 4):
+        target = here.along_a(n // 4, n % 4, 0)
+        at = pl.multiple_of(target[0] // 2 * OWN * SI, 8)
         copies.append(
             send_part(
-                part.at[s, target[0]], into.at[s, n], send_sems.at[s, n],
-                recv_sems.at[s, n], target,
+                part.at[pl.ds(at, OWN * SI), :], into.at[n], send_sems.at[n],
+                recv_sems.at[n], target,
             )
         )
     return copies
@@ -410,8 +408,8 @@
     t_hbm, g_hbm, h_hbm, q_hbm, r_hbm, u_hbm, ve_hbm, oe_hbm, se_hbm,
     row_out, col_out,
     t_ref, g_in, h_in, q_in, r_in, u_in, ve_ref, oe_ref, se_ref,
-    q_ref, amp, rows, cols, a_ref, g2, r2, bdh, bdu, p_ref, c_ref, yr, yc, res, wide, held,
-    row_part, col_part, row_into, col_into, last,
+    q_ref, amp, rows, cols, a_ref, g2, r2, bdh, bdu, p_ref, c_ref, yr, yc, res, held,
+    row_part, col_part, row_into, col_into, twin_into, col_sum,
     in_sems, gather_sems, row_sems, col_sems, out_row_sems, out_col_sems, sum_row_sems,
     sum_col_sems,
 ):
@@ -481,7 +479,7 @@
             net.got_col(kind, d)
     spread(cols, functools.partial(put_cols, bdh, bdu))
     base = pair_energy(here, ve_ref)
-    row_sums, col_sums = [], []
+    row_sums = []
     for group in range(2):
         for k in ORDER[group * HALF : (group + 1) * HALF]:
             net.got_row(1, k)
@@ -498,19 +496,22 @@
             if group == 0:
                 col_first(s, turned, yc, held)
                 continue
-            col_residual(s, turned, yc, held, res, wide, col_part.at[s])
-            col_sums += scatter_cols(
-                here, s, col_part, col_into, out_col_sems, sum_col_sems
-            )
+            col_residual(s, turned, yc, held, res, col_part)
+    twin = send_part(
+        col_part.at[1 - here.core], twin_into, out_col_sems.at[0], sum_col_sems.at[0],
+        here.along_a(0, 0, 1),
+    )
     for copy in net.sent:
         copy.wait_send()
-    for s in range(NC):
-        total = col_part[s, here.a]
-        for n in range(1, GROUP):
-            col_sums[s * (GROUP - 1) + n - 1].wait_recv()
-            total = total + col_into[s, n]
-        last[pl.ds(s, USED, stride=NC), :] = total
-    col_out[...] = last[...]
+    twin.wait_recv()
+    col_sum[...] = col_part[here.core] + twin_into[...]
+    col_sums = scatter_cols(here, col_sum, col_into, out_col_sems, sum_col_sems)
+    total = col_sum[pl.ds(pl.multiple_of(here.a // 2 * OWN * SI, 8), OWN * SI), :]
+    for copy in col_sums:
+        copy.wait_recv()
+    for n in range(1, 8):
+        total = total + col_into[n]
+    col_out[...] = total
     at = ORDER.index(0)
     total = row_part[at // HALF, at % HALF * OWN * SI : (at % HALF + 1) * OWN * SI, :]
     for copy in row_sums:
@@ -518,7 +519,7 @@
     for n in range(1, GROUP):
         total = total + row_into[n]
     row_out[...] = total
-    for copy in row_sums + col_sums:
+    for copy in row_sums + col_sums + [twin]:
         copy.wait_send()
 
 
@@ -567,21 +568,21 @@
             pltpu.VMEM((160, JK * NO), BF16),
             pltpu.VMEM((SI * 400, NO), BF16),
             pltpu.VMEM((OT * 64, NO), F32),
-            pltpu.VMEM((GROUP * PART, NO), F32),
             pltpu.VMEM((SI, NO, NO), F32),
             pltpu.VMEM((2, 2 * HALF * OWN * SI, NO), F32),
-            pltpu.VMEM((NC, GROUP, USED, NO), F32),
+            pltpu.VMEM((2, 8 * OWN * SI, NO), F32),
             pltpu.VMEM((GROUP, OWN * SI, NO), F32),
-            pltpu.VMEM((NC, GROUP, USED, NO), F32),
-            pltpu.VMEM((NC * USED, NO), F32),
+            pltpu.VMEM((8, OWN * SI, NO), F32),
+            pltpu.VMEM((8 * OWN * SI, NO), F32),
+            pltpu.VMEM((8 * OWN * SI, NO), F32),
             dma((9,)),
             dma((30,)),
             dma((2, 8)),
             dma((4, 4)),
             dma((GROUP,)),
-            dma((NC, GROUP)),
+            dma((8,)),
             dma((GROUP,)),
-            dma((NC, GROUP)),
+            dma((8,)),
         ],
         compiler_params=pltpu.CompilerParams(
             collective_id=0, has_side_effects=True, vmem_limit_bytes=56 * 2**20

time: 38 us -> 35.7 us (0.939)
  Pallas kernels: 36.7 us -> 34.3 us
    pallas_call x1, Pallas kernels: 36.7 us -> 34.3 us  [on_device(): pl.pallas_call(whole_body, out_shape=(out, out), in_specs=[pl.BlockSpec(m...]
where the time goes in v5:
time: 35.7 us; the launch traced here: 35.6 us
  Pallas kernels  34.3 us (96%)
  between operations  0.64 us (2%)
  other arithmetic  0.62 us (2%)
    pallas_call x1, Pallas kernels, on_device(): pl.pallas_call(whole_body, out_shape=(out, out), in_specs=[pl.BlockSpec(m...  34.3 us

profile of v5, /device:TPU:1, one launch (start us, length us, event | category | flops | bytes accessed | tf_op | source)
XLA Modules:
  0.0 35.6 jit_solution(17725241795803482269)
XLA Ops:
  0.6 34.3 %shard_map.104 = (f32[40,128]{1,0:T(8,128)S(1)}, f32[40,128]{1,0:T(8,128)S(1)}) custom-call(bf16[64,5,64,128]{3,2,1,0:T(8,128)(2,1)} %bitcast.14, bf16[4,3200]{1,0:T(4,128)(2,1)} %g_hbm.1, bf16[4,3200]{1,0:T(4,128)(2,1)} %h_hbm.1, bf16[2,3200]{1,0:T(2,128)(2,1)} %q_hbm.1, bf16[40,128]{1,0:T(8,128)(2,1)} %bitcast.17, bf16[40,128]{1,0:T(8,128)(2,1)} %bitcast.18, ...), custom_call_target="tpu_custom_call" | custom-call | tf_op jit(solution)/shard_map/pallas_call | solution.py:550
  35.0 0.6 %broadcast_multiply_fusion = (f32[40,128]{1,0:T(8,128)}, f32[40,128]{1,0:T(8,128)}) fusion(f32[40,128]{1,0:T(8,128)S(1)} %get-tuple-element.5, f32[40,128]{1,0:T(8,128)S(1)} %get-tuple-element.4), kind=kLoop, calls=%fused_computation | loop fusion | flops 10240 | bytes 81920 | tf_op jit(solution)/shard_map/mul | solution.py:592

commit v6 on v5

--- a/solution.py
+++ b/solution.py
@@ -458,21 +458,22 @@
     for d in range(1, 4):
         net.got_col(0, d)
         net.twin_col(0, d)
-    compute_a(here, t_ref, q_ref, a_ref, 2, 2)
+    compute_a(here, t_ref, q_ref, a_ref, 2, 1)
     for k in others[2:4]:
         net.got_row(0, k)
         net.across_x(k)
     for d in range(1, 4):
         net.got_col(1, d)
         net.twin_col(1, d)
-    compute_a(here, t_ref, q_ref, a_ref, 4, 2)
+    compute_a(here, t_ref, q_ref, a_ref, 3, 1)
     for k in others[4:6]:
         net.got_row(0, k)
         net.across_x(k)
-    compute_a(here, t_ref, q_ref, a_ref, 6, 2)
+    compute_a(here, t_ref, q_ref, a_ref, 4, 1)
     for k in others[6:]:
         net.got_row(0, k)
         net.across_x(k)
+    compute_a(here, t_ref, q_ref, a_ref, 5, 3)
     clear_off(bdh, bdu)
     for kind in (2, 3):
         for d in range(4):

time: 35.7 us -> 35.4 us (level)
  no operation moved by 1% of the time
where the time goes in v6:
time: 35.4 us; the launch traced here: 35.3 us
  Pallas kernels  34 us (96%)
  between operations  0.64 us (2%)
  other arithmetic  0.62 us (2%)
    pallas_call x1, Pallas kernels, on_device(): pl.pallas_call(whole_body, out_shape=(out, out), in_specs=[pl.BlockSpec(m...  34 us

profile of v6, /device:TPU:1, one launch (start us, length us, event | category | flops | bytes accessed | tf_op | source)
XLA Modules:
  0.0 35.3 jit_solution(1665770753584747524)
XLA Ops:
  0.6 34.0 %shard_map.104 = (f32[40,128]{1,0:T(8,128)S(1)}, f32[40,128]{1,0:T(8,128)S(1)}) custom-call(bf16[64,5,64,128]{3,2,1,0:T(8,128)(2,1)} %bitcast.14, bf16[4,3200]{1,0:T(4,128)(2,1)} %g_hbm.1, bf16[4,3200]{1,0:T(4,128)(2,1)} %h_hbm.1, bf16[2,3200]{1,0:T(2,128)(2,1)} %q_hbm.1, bf16[40,128]{1,0:T(8,128)(2,1)} %bitcast.17, bf16[40,128]{1,0:T(8,128)(2,1)} %bitcast.18, ...), custom_call_target="tpu_custom_call" | custom-call | tf_op jit(solution)/shard_map/pallas_call | solution.py:551
  34.6 0.6 %broadcast_multiply_fusion = (f32[40,128]{1,0:T(8,128)}, f32[40,128]{1,0:T(8,128)}) fusion(f32[40,128]{1,0:T(8,128)S(1)} %get-tuple-element.5, f32[40,128]{1,0:T(8,128)S(1)} %get-tuple-element.4), kind=kLoop, calls=%fused_computation | loop fusion | flops 10240 | bytes 81920 | tf_op jit(solution)/shard_map/mul | solution.py:593
